TPU v7x, 128 devices: a whole 4x4x4 slice. The times are simulated.
128 devices in a mesh: gx: 16 (over z, y), gy: 8 (over x, core).
Axes of the slice: x: 4, y: 4, z: 4, core: 2. Of those that a mesh axis runs over, the one named last changes fastest.
Arguments:
- activations: bfloat16 [128, 16, 8192], P('gy', None, 'gx'), may hold values from -80 to 80
- norm_gain: bfloat16 [8192], P('gx'), may hold values from 0.099609375 to 1.8984375
- query_weight: bfloat16 [8192, 8192], P('gx', 'gy'), may hold values from -0.0625 to 0.0625
- key_weight: bfloat16 [8192, 1024], P('gx', 'gy'), may hold values from -0.0625 to 0.0625
- value_weight: bfloat16 [8192, 1024], P('gx', 'gy'), may hold values from -0.0625 to 0.0625
- out_weight: bfloat16 [8192, 8192], P('gy', 'gx'), may hold values from -0.0625 to 0.0625
- key_cache: bfloat16 [128, 4096, 1024], P(('gx', 'gy')), may hold values from -250 to 250
- value_cache: bfloat16 [128, 4096, 1024], P(('gx', 'gy')), may hold values from -16 to 16
- lengths: int32 [128], P(('gx', 'gy')), may hold values from 1 to 4096, as said below
- positions: int32 [128], P(('gx', 'gy')), may hold values from 0 to 8191
Outputs:
- mixed: bfloat16 [128, 16, 8192], P('gy', None, 'gx')
Inputs may be any that keep to these rules, and one draw needn't show every extreme that they name: `lengths`: some sequence has length 1 and some has length 4096 in every draw.
All inputs are finite; a program needn't handle non-finite values.
Results may differ from a plain program's by a relative error of at most 0.019.
The roundings to bfloat16 on the way count: a program that leaves them out, or rounds other values in their place, can miss the bound.
Values may be sent and summed in bfloat16 or wider, within the bound.
A program may use at most 192 MiB of HBM per device.

v0:
```python
import math

import jax
import jax.numpy as jnp
from jax import lax
from jax.sharding import PartitionSpec as P

D = 8192
HEADS = 64
KV = 8
HD = 128


def rotate(vector, places):
    halfway = vector.shape[-1] // 2
    frequency = jnp.exp(
        jnp.arange(halfway, dtype=jnp.float32) * (-2.0 * math.log(500000.0) / vector.shape[-1])
    )
    angles = places.astype(jnp.float32)[..., None] * frequency
    cosine = jnp.cos(angles)[..., None, :]
    sine_part = jnp.sin(angles)[..., None, :]
    first_half = vector[..., :halfway]
    second = vector[..., halfway:]
    return jnp.concatenate(
        [first_half * cosine - second * sine_part, second * cosine + first_half * sine_part],
        axis=-1,
    )


def attend_row(query, fresh_keys, fresh_values, cache_keys, cache_values, length):
    drafts = query.shape[0]
    slots = cache_keys.shape[0]
    group_size = HEADS // KV
    query_heads = query.reshape(drafts, KV, group_size, HD)
    keys_old = cache_keys.reshape(slots, KV, HD)
    values_old = cache_values.reshape(slots, KV, HD)
    keys_new = fresh_keys.reshape(drafts, KV, HD)
    values_new = fresh_values.reshape(drafts, KV, HD)
    scaling = HD ** (-0.5)
    cached_scores = (
        jnp.einsum("tkgd,ckd->kgtc", query_heads, keys_old, preferred_element_type=jnp.float32)
        * scaling
    )
    fresh_scores = (
        jnp.einsum("tkgd,skd->kgts", query_heads, keys_new, preferred_element_type=jnp.float32)
        * scaling
    )
    visible = jnp.arange(slots, dtype=jnp.int32) < length
    causal = (
        jnp.arange(drafts, dtype=jnp.int32)[None, :] <= jnp.arange(drafts, dtype=jnp.int32)[:, None]
    )
    highest = jnp.maximum(
        jnp.max(jnp.where(visible, cached_scores, -1e30), axis=-1),
        jnp.max(jnp.where(causal, fresh_scores, -1e30), axis=-1),
    )
    cached_weights = jnp.where(visible, jnp.exp(cached_scores - highest[..., None]), 0.0)
    fresh_weights = jnp.where(causal, jnp.exp(fresh_scores - highest[..., None]), 0.0)
    totals = jnp.sum(cached_weights, axis=-1) + jnp.sum(fresh_weights, axis=-1)
    blended = jnp.einsum(
        "kgtc,ckd->tkgd",
        cached_weights.astype(jnp.bfloat16),
        values_old,
        preferred_element_type=jnp.float32,
    )
    blended = blended + jnp.einsum(
        "kgts,skd->tkgd",
        fresh_weights.astype(jnp.bfloat16),
        values_new,
        preferred_element_type=jnp.float32,
    )
    result = blended / jnp.transpose(totals, (2, 0, 1))[..., None]
    return result.reshape(drafts, HEADS * HD).astype(jnp.bfloat16)


def shards(
    activations,
    norm_gain,
    query_weight,
    key_weight,
    value_weight,
    out_weight,
    key_cache,
    value_cache,
    lengths,
    positions,
):
    gathered = lax.all_gather(activations, "gy", axis=0, tiled=True)
    block_rows = gathered.shape[0] // lax.axis_size("gx")
    widened = gathered.astype(jnp.float32)
    squares = jnp.sum(widened * widened, axis=-1)
    scaled = (widened * norm_gain.astype(jnp.float32)).astype(jnp.bfloat16)
    query_part = jnp.einsum("btd,df->btf", scaled, query_weight, preferred_element_type=jnp.float32)
    key_part = jnp.einsum("btd,df->btf", scaled, key_weight, preferred_element_type=jnp.float32)
    value_part = jnp.einsum("btd,df->btf", scaled, value_weight, preferred_element_type=jnp.float32)
    totals = lax.psum(squares, "gx")
    query_sum, key_sum, value_sum = (
        lax.psum_scatter(query_part, "gx", scatter_dimension=0, tiled=True),
        lax.psum_scatter(key_part, "gx", scatter_dimension=0, tiled=True),
        lax.psum_scatter(value_part, "gx", scatter_dimension=0, tiled=True),
    )
    own_totals = lax.dynamic_slice_in_dim(totals, lax.axis_index("gx") * block_rows, block_rows, 0)
    rms_inv = lax.rsqrt(own_totals / D + 1e-05)[..., None]
    drafts = query_sum.shape[1]
    row_places = lax.all_gather(positions, "gy", axis=0, tiled=True)
    places = row_places[:, None] + jnp.arange(drafts, dtype=jnp.int32)[None, :]
    query_heads = query_sum.shape[-1] // HD
    key_heads = key_sum.shape[-1] // HD
    query_rot = rotate((query_sum * rms_inv).reshape(block_rows, drafts, query_heads, HD), places)
    query_rot = query_rot.reshape(block_rows, drafts, query_heads * HD).astype(jnp.bfloat16)
    key_rot = rotate((key_sum * rms_inv).reshape(block_rows, drafts, key_heads, HD), places)
    key_rot = key_rot.reshape(block_rows, drafts, key_heads * HD).astype(jnp.bfloat16)
    value_new = (value_sum * rms_inv).astype(jnp.bfloat16)
    query_rows, key_rows, value_rows = (
        lax.all_to_all(query_rot, "gy", split_axis=0, concat_axis=2, tiled=True),
        lax.all_to_all(key_rot, "gy", split_axis=0, concat_axis=2, tiled=True),
        lax.all_to_all(value_new, "gy", split_axis=0, concat_axis=2, tiled=True),
    )
    attended = lax.map(
        lambda packet: attend_row(*packet),
        (query_rows, key_rows, value_rows, key_cache, value_cache, lengths),
    )
    regrouped = lax.all_to_all(attended, "gy", split_axis=2, concat_axis=0, tiled=True)
    terms = jnp.einsum(
        "btf,fd->btd",
        lax.all_gather(regrouped, "gx", axis=0, tiled=True),
        out_weight,
        preferred_element_type=jnp.float32,
    )
    mixed = lax.psum_scatter(terms.astype(jnp.bfloat16), "gy", scatter_dimension=0, tiled=True)
    return mixed


def solution(mesh):
    return jax.shard_map(
        shards,
        mesh=mesh,
        in_specs=(
            P("gy", None, "gx"),
            P("gx"),
            P("gx", "gy"),
            P("gx", "gy"),
            P("gx", "gy"),
            P("gy", "gx"),
            P(("gx", "gy"), None, None),
            P(("gx", "gy"), None, None),
            P(("gx", "gy")),
            P(("gx", "gy")),
        ),
        out_specs=P("gy", None, "gx"),
        check_vma=False,
    )
```

profile of v0, /device:TPU:1, one launch (start us, length us, event | category | flops | bytes accessed | tf_op | source)
XLA Modules:
  0.0 514.6 jit_solution(11518395692839205375)
XLA Ops:
  6.5 0.7 all-gather.4.cloned.1.call-update
  7.3 0.0 reduce-scatter.7.cloned.1.call-start
  7.3 0.7 convert_element_type.54
  8.0 29.9 %all-gather.4.cloned.1.call-done = bf16[128,16,512]{2,1,0:T(8,128)(2,1)} async-done(((bf16[16,16,512]{2,1,0:T(8,128)(2,1)}), bf16[128,16,512]{2,1,0:T(8,128)(2,1)}) %all-gather.4.cloned.1.call-update) | async-done | bytes 2097168 | tf_op jit(solution)/shard_map/all_gather | solution.py:87
  37.9 2.3 fusion.15
  40.1 4.3 fusion.23
  44.5 0.0 reduce-scatter.7.cloned.1.call-update
  44.5 0.0 reduce-scatter.9.cloned.1.call-start
  44.6 3.4 fusion.21
  47.9 0.0 reduce-scatter.9.cloned.1.call-update
  48.0 0.0 reduce-scatter.5.cloned.1.call-start
  48.0 7.1 %fusion.25 = f32[128,16,1024]{2,0,1:T(8,128)} fusion(bf16[128,16,512]{2,1,0:T(8,128)(2,1)S(1)} %get-tuple-element.20, bf16[512,1024]{1,0:T(8,128)(2,1)S(1)} %copy-done), kind=kOutput, calls=%fused_computation.26 | convolution fusion | flops 2147483648 | bytes 11534336 | tf_op jit(solution)/shard_map/btd,df->btf/dot_general | solution.py:92
  55.1 0.0 reduce-scatter.5.cloned.1.call-update
  55.8 0.6 dynamic-slice
  56.3 0.8 dynamic-update-slice
  57.1 6.5 %all-reduce = s32[8]{0:T(128)S(1)} all-reduce(s32[8]{0:T(128)S(1)} %dynamic-update-slice), channel_id=1, replica_groups=mesh['gx'=16,'gy'=8] {'gy'}, use_global_device_ids=true, to_apply=%add | all-reduce | flops 8 | bytes 64
  63.6 0.1 copy.83
  64.3 8.8 %copy.112 = bf16[512,8,8,128]{3,2,1,0:T(8,128)(2,1)} copy(bf16[512,8,8,128]{3,1,2,0:T(8,128)(2,1)} %bitcast.119) | data formatting | bytes 16777216
  73.1 8.8 %copy.113 = bf16[512,8,8,128]{3,2,1,0:T(8,128)(2,1)} copy(bf16[512,8,8,128]{3,1,2,0:T(8,128)(2,1)} %bitcast.120) | data formatting | bytes 16777216
  82.0 0.3 multiply_cosine_fusion.1
  82.3 60.8 %psum.7 = f32[128,16]{1,0:T(8,128)S(1)} all-reduce(f32[128,16]{1,0:T(8,128)S(1)} %get-tuple-element.19), channel_id=1, replica_groups=mesh['gx'=16,'gy'=8] {'gx'}, use_global_device_ids=true, to_apply=%region_2.0 | all-reduce | flops 2048 | bytes 16384 | tf_op jit(solution)/shard_map/psum | solution.py:95
  143.1 0.1 copy.81
  143.1 48.8 %reduce-scatter.9.cloned.1.call-done = f32[8,16,128]{2,0,1:T(8,128)} async-done(((f32[128,16,128]{2,0,1:T(8,128)}), f32[8,16,128]{2,0,1:T(8,128)}) %reduce-scatter.9.cloned.1.call-update) | async-done | bytes 65552 | tf_op jit(solution)/shard_map/reduce_scatter | solution.py:99
  192.0 1.0 multiply_convert_fusion
  192.9 87.1 %reduce-scatter.5.cloned.1.call-done = f32[8,16,1024]{2,0,1:T(8,128)} async-done(((f32[128,16,1024]{2,0,1:T(8,128)}), f32[8,16,1024]{2,0,1:T(8,128)}) %reduce-scatter.5.cloned.1.call-update) | async-done | bytes 524304 | tf_op jit(solution)/shard_map/reduce_scatter | solution.py:97
  280.0 1.1 multiply_bitcast_fusion
  281.2 0.2 fusion.55
  281.4 0.3 subtract_convert_fusion
  281.7 0.1 pad_maximum_fusion
  281.8 0.8 convert_element_type.57
  282.6 6.1 %all-to-all-start = ((bf16[8,16,1024]{2,1,0:T(8,128)(2,1)}), bf16[8,16,1024]{2,1,0:T(8,128)(2,1)S(1)}, u32[]{:S(2)}, u32[]{:S(2)}) async-start(bf16[8,16,1024]{2,1,0:T(8,128)(2,1)} %convert_element_type.57), calls=%async_computation.1 | async-start | bytes 524288 | tf_op jit(solution)/shard_map/all_to_all | solution.py:114
  288.7 0.3 fusion.48
  289.1 0.1 maximum_bitcast_fusion
  289.2 0.6 copy.88
  289.8 0.6 copy.94
  290.4 4.9 all-to-all-done
  295.2 4.3 all-to-all-start.1
  299.6 13.7 %fusion = (f32[8,8,16]{1,2,0:T(8,128)S(1)}, f32[8,16,8,4096]{3,2,1,0:T(8,128)}) fusion(pred[4096]{0:T(1024)(128)(4,1)S(1)} %iota_compare_fusion, bf16[16,8,8,128]{3,2,0,1:T(8,128)(2,1)S(1)} %bitcast.122, bf16[4096,8,128,1]{2,1,0,3:T(8,128)(2,1)} %bitcast.116), kind=kOutput, calls=%fused_computation.2 | convolution fusion | flops 1086323712 | bytes 25436160 | tf_op jit(solution)/shard_map/while/body/eval_jaxpr/tkgd,ckd->kgtc/dot_general | solution.py:41
  313.3 0.1 copy.90
  313.3 4.8 all-to-all-start.2
  318.2 0.7 select_reduce_fusion
  318.9 0.1 copy.91
  319.0 0.2 fusion.38
  319.2 0.1 copy.96
  319.3 8.2 %fusion.3 = f32[8,8,16]{1,2,0:T(8,128)S(1)} fusion(f32[8,16,8,4096]{3,2,1,0:T(8,128)} %get-tuple-element.44, f32[8,8,16]{1,2,0:T(8,128)S(1)} %copy.91, pred[4096]{0:T(1024)(128)(4,1)S(1)} %iota_compare_fusion), kind=kLoop, calls=%fused_computation.5 | loop fusion | flops 16776192 | bytes 16789504 | tf_op jit(solution)/shard_map/while/body/eval_jaxpr/reduce_sum | solution.py:58
  327.5 11.9 %fusion.30 = f32[16,8,8,128]{3,2,0,1:T(8,128)S(1)} fusion(bf16[4096,8,128,1]{2,1,0,3:T(8,128)(2,1)} %bitcast.121, f32[8,16,8,4096]{3,2,1,0:T(8,128)} %get-tuple-element.44, f32[8,8,16]{1,2,0:T(8,128)S(1)} %copy.91, pred[4096]{0:T(1024)(128)(4,1)S(1)} %iota_compare_fusion), kind=kOutput, calls=%fused_computation.33 | convolution fusion | flops 1090519040 | bytes 25698304 | tf_op jit(solution)/shard_map/while/body/eval_jaxpr/kgtc,ckd->tkgd/dot_general | solution.py:59
  339.4 0.2 copy.95
  339.7 0.2 fusion.35
  339.9 0.1 copy.97
  340.0 0.1 convert_element_type.63
  340.1 6.7 %copy.98 = bf16[1,16,8192]{1,0,2:T(2,128)(2,1)} copy(bf16[1,16,8192]{2,1,0:T(8,128)(2,1)S(1)} %convert_element_type.63) | data formatting | bytes 524288 | tf_op jit(solution)/shard_map/while/body/eval_jaxpr/convert_element_type | solution.py:72
  346.8 0.5 broadcast.77
  347.3 45.2 %reduce = bf16[8192,16]{1,0:T(8,128)(2,1)S(1)} reduce(bf16[8192,1,16]{2,1,0:T(2,128)(2,1)} %bitcast.117, bf16[]{:T(256)} %broadcast.77), dimensions={1}, to_apply=%bitcast.108.reduce_sub_computation | reduce | bytes 524290
  392.5 2.2 reshape.116
  394.7 11.1 %all_to_all.63 = bf16[8,2,8192]{2,1,0:T(2,128)(2,1)S(1)} all-to-all(bf16[8,2,8192]{2,1,0:T(2,128)(2,1)S(1)} %reshape.116), channel_id=1, replica_groups=mesh['gx'=16,'gy'=8] {'gy'}, dimensions={0} | all-to-all | bytes 524288 | tf_op jit(solution)/shard_map/all_to_all | solution.py:122
  405.8 5.0 reshape.117
  410.9 7.9 %copy.99 = bf16[1,16,8192]{2,1,0:T(8,128)(2,1)S(1)} copy(bf16[1,16,8192]{1,0,2:T(2,128)(2,1)} %bitcast.118) | data formatting | bytes 524288 | tf_op jit(solution)/shard_map/all_to_all | solution.py:122
  418.7 0.2 copy.114
  418.9 0.7 bitcast_bitcast_fusion
  419.6 0.0 reduce-scatter.11.cloned.1.call-start
  419.7 49.6 %all-gather.6.cloned.1.call-done = bf16[128,1,16,1024]{3,0,2,1:T(8,128)(2,1)} async-done(((bf16[8,1,16,1024]{3,0,2,1:T(8,128)(2,1)}), bf16[128,1,16,1024]{3,0,2,1:T(8,128)(2,1)}) %all-gather.6.cloned.1.call-update) | async-done | bytes 4194320 | tf_op jit(solution)/shard_map/all_gather | solution.py:125
  469.3 6.2 %fusion.18 = bf16[128,16,512]{2,0,1:T(8,128)(2,1)} fusion(bf16[128,1,16,1024]{3,0,2,1:T(8,128)(2,1)} %all-gather.6.cloned.1.call-done, bf16[1024,512]{1,0:T(8,128)(2,1)} %param.15), kind=kOutput, calls=%fused_computation.21 | convolution fusion | flops 2148532224 | bytes 7340032 | tf_op jit(solution)/shard_map/btf,fd->btd/dot_general | solution.py:123
  475.5 30.4 %reduce-scatter.11.cloned.1.call-done = bf16[16,16,512]{2,0,1:T(8,128)(2,1)} async-done(((bf16[128,16,512]{2,0,1:T(8,128)(2,1)}), bf16[16,16,512]{2,0,1:T(8,128)(2,1)}) %reduce-scatter.11.cloned.1.call-update) | async-done | bytes 262160 | tf_op jit(solution)/shard_map/reduce_scatter | solution.py:129
  505.9 1.8 copy.100
  (24 shorter events, 0.2 us)
Async XLA Ops:
  6.5 41.5 %copy-start = (bf16[512,1024]{1,0:T(8,128)(2,1)S(1)}, bf16[512,1024]{1,0:T(8,128)(2,1)}, u32[]{:S(2)}) copy-start(bf16[512,1024]{1,0:T(8,128)(2,1)} %param.12) | copy-start | bytes 3145732
  6.5 38.0 %copy-start.2 = (bf16[512,128]{1,0:T(8,128)(2,1)S(1)}, bf16[512,128]{1,0:T(8,128)(2,1)}, u32[]{:S(2)}) copy-start(bf16[512,128]{1,0:T(8,128)(2,1)} %param.14) | copy-start | bytes 393220
  6.5 31.3 %all-gather.4.cloned.1.call-start = ((), (), s32[]{:S(2)}) async-start(), calls=%async_computation.8 | async-start | bytes 2359296 | tf_op jit(solution)/shard_map/all_gather | solution.py:87
  7.3 135.9 %reduce-scatter.7.cloned.1.call-start = ((), (), s32[]{:S(2)}) async-start(), calls=%async_computation.10 | async-start | bytes 1114112 | tf_op jit(solution)/shard_map/reduce_scatter | solution.py:98
  44.5 147.5 %reduce-scatter.9.cloned.1.call-start = ((), (), s32[]{:S(2)}) async-start(), calls=%async_computation.11 | async-start | bytes 1114112 | tf_op jit(solution)/shard_map/reduce_scatter | solution.py:99
  48.0 232.1 %reduce-scatter.5.cloned.1.call-start = ((), (), s32[]{:S(2)}) async-start(), calls=%async_computation.9 | async-start | bytes 8912896 | tf_op jit(solution)/shard_map/reduce_scatter | solution.py:97
  55.1 0.7 copy-start.3
  282.6 12.6 %all-to-all-start = ((bf16[8,16,1024]{2,1,0:T(8,128)(2,1)}), bf16[8,16,1024]{2,1,0:T(8,128)(2,1)S(1)}, u32[]{:S(2)}, u32[]{:S(2)}) async-start(bf16[8,16,1024]{2,1,0:T(8,128)(2,1)} %convert_element_type.57), calls=%async_computation.1 | async-start | bytes 524288 | tf_op jit(solution)/shard_map/all_to_all | solution.py:114
  295.2 18.1 %all-to-all-start.1 = ((bf16[8,16,128]{2,1,0:T(8,128)(2,1)}), bf16[8,16,128]{2,1,0:T(8,128)(2,1)S(1)}, u32[]{:S(2)}, u32[]{:S(2)}) async-start(bf16[8,16,128]{2,1,0:T(8,128)(2,1)} %copy.88), calls=%async_computation.3 | async-start | bytes 65536 | tf_op jit(solution)/shard_map/all_to_all | solution.py:115
  313.3 26.3 %all-to-all-start.2 = ((bf16[8,16,128]{2,1,0:T(8,128)(2,1)}), bf16[8,16,128]{2,1,0:T(8,128)(2,1)S(1)}, u32[]{:S(2)}, u32[]{:S(2)}) async-start(bf16[8,16,128]{2,1,0:T(8,128)(2,1)} %copy.94), calls=%async_computation.5 | async-start | bytes 65536 | tf_op jit(solution)/shard_map/all_to_all | solution.py:116
  318.2 151.1 %all-gather.6.cloned.1.call-start = ((), (), s32[]{:S(2)}) async-start(), calls=%async_computation.13 | async-start | bytes 4456448 | tf_op jit(solution)/shard_map/all_gather | solution.py:125
  419.6 88.1 %copy-start.1 = (bf16[512,1024]{1,0:T(8,128)(2,1)S(1)}, bf16[512,1024]{1,0:T(8,128)(2,1)}, u32[]{:S(2)}) copy-start(bf16[512,1024]{1,0:T(8,128)(2,1)} %param.12) | copy-start | bytes 3145732
  419.6 86.3 %reduce-scatter.11.cloned.1.call-start = ((), (), s32[]{:S(2)}) async-start(), calls=%async_computation.12 | async-start | bytes 2359296 | tf_op jit(solution)/shard_map/reduce_scatter | solution.py:129
Sparse Core Ops, SparseCore 0:
  9.1 28.7 all-gather.3
  44.6 71.5 reduce-scatter.6
  119.7 72.2 reduce-scatter.8
  195.2 84.7 reduce-scatter.4
  419.7 49.5 all-gather.5
  475.6 30.2 reduce-scatter.10
where the time goes:
time: 518 us; the launch traced here: 515 us
  waiting for transfers between devices  252 us (49%)
  blocking collectives  78.4 us (15%)
  other arithmetic  59.9 us (12%)
  matrix products  47.5 us (9%)
  local copies, waits for them, and re-layouts  47 us (9%)
  starting transfers between devices  15.4 us (3%)
  between operations  15 us (3%)
    reduce_scatter x1, waiting for transfers between devices, shards(): lax.psum_scatter(query_part, 'gx', scatter_dimension=0, tiled=True)  87.1 us
    psum x1, blocking collectives, shards(): totals = lax.psum(squares, 'gx')  60.8 us
    all_gather x1, waiting for transfers between devices, shards(): lax.all_gather(regrouped, 'gx', axis=0, tiled=True)  49.6 us
    reduce_scatter x1, waiting for transfers between devices, shards(): lax.psum_scatter(value_part, 'gx', scatter_dimension=0, tiled=True)  48.8 us
    unnamed x1, other arithmetic  45.2 us
    reduce_scatter x1, waiting for transfers between devices, shards(): lax.psum_scatter(terms.astype(jnp.bfloat16), 'gy', scatter_dimension=0, t...  30.4 us
    all_gather x1, waiting for transfers between devices, shards(): gathered = lax.all_gather(activations, 'gy', axis=0, tiled=True)  29.9 us
    unnamed x18, local copies, waits for them, and re-layouts  26.9 us
  transfers between devices with their start and end apart: 9, of which 6 were waited for; matrix products, arithmetic and copies ran while one was open for 13% of the time, Pallas kernels for 0%

commit v1 on v0

v1 whole, which is shorter than its diff:
```python
import math

import jax
import jax.numpy as jnp
from jax import lax
from jax.experimental import pallas as pl
from jax.experimental.pallas import tpu as pltpu
from jax.sharding import PartitionSpec as P

D = 8192
HD = 128
KV = 8
CTX = 4096
DRAFT = 16
QA = 512
QB = 768
MESH = pl.DeviceIdType.MESH
F32 = jnp.float32
BF = jnp.bfloat16


def wrap(value, size=4):
    return lax.rem(value + size, size)


class Place:
    def __init__(self):
        gx, gy = lax.axis_index("gx"), lax.axis_index("gy")
        self.gx, self.gy = gx, gy
        self.z, self.y = lax.div(gx, 4), lax.rem(gx, 4)
        self.x, self.c = lax.div(gy, 2), lax.rem(gy, 2)
        self.sibling = (gx, gy + 1 - 2 * self.c)

    def at_x(self, step):
        return (self.gx, wrap(self.x + step) * 2 + self.c)

    def at_y(self, step):
        return (self.z * 4 + wrap(self.y + step), self.gy)

    def at_z(self, step):
        return (wrap(self.z + step) * 4 + self.y, self.gy)

    def at_gy(self, step):
        return (self.gx, wrap(self.gy + step, 8))


class Net:
    def __init__(self, send_sem, recv_sem):
        self.send_sem, self.recv_sem = send_sem, recv_sem
        self.made = []

    def send(self, src, dst, device):
        index = len(self.made)
        copy = pltpu.make_async_remote_copy(
            src_ref=src,
            dst_ref=dst,
            send_sem=self.send_sem.at[index],
            recv_sem=self.recv_sem.at[index],
            device_id=device,
            device_id_type=MESH,
        )
        copy.start()
        self.made.append(copy)
        return copy

    def drain(self):
        for copy in self.made:
            copy.wait_send()


def greet(devices):
    barrier = pltpu.get_barrier_semaphore()
    for device in devices:
        pl.semaphore_signal(barrier, inc=1, device_id=device, device_id_type=MESH)
    pl.semaphore_wait(barrier, len(devices))


class RingSum:
    def __init__(self, net, get, plus, minus, bufs, lead, rows):
        self.net, self.get, self.plus, self.minus = net, get, plus, minus
        self.rows, self.half = rows, rows // 2
        self.so, self.sp, self.sm, self.rom, self.rop, self.rdm, self.rdp, self.kp, self.km = [
            buf.at[lead] for buf in bufs
        ]

    def start(self):
        h, r, net = self.half, self.rows, self.net
        lo, hi = pl.ds(0, h), pl.ds(h, h)
        self.so[...] = self.get(2).astype(BF)
        self.c_om = net.send(self.so.at[lo], self.rom, self.plus)
        self.c_op = net.send(self.so.at[hi], self.rop, self.minus)
        part = self.get(1)
        self.kp[...] = part[:h]
        self.sp[hi] = part[h:].astype(BF)
        self.c_dm1 = net.send(self.sp.at[hi], self.rdm.at[hi], self.plus)
        part = self.get(3)
        self.km[...] = part[h:]
        self.sm[lo] = part[:h].astype(BF)
        self.c_dp1 = net.send(self.sm.at[lo], self.rdp.at[lo], self.minus)

    def mid(self):
        h, net = self.half, self.net
        lo, hi = pl.ds(0, h), pl.ds(h, h)
        self.c_om.wait_recv()
        self.sp[lo] = (self.kp[...] + self.rom[...].astype(F32)).astype(BF)
        self.c_dm2 = net.send(self.sp.at[lo], self.rdm.at[lo], self.plus)
        self.c_op.wait_recv()
        self.sm[hi] = (self.km[...] + self.rop[...].astype(F32)).astype(BF)
        self.c_dp2 = net.send(self.sm.at[hi], self.rdp.at[hi], self.minus)

    def finish(self):
        own = self.get(0)
        for copy in (self.c_dm1, self.c_dp1, self.c_dm2, self.c_dp2):
            copy.wait_recv()
        return own + self.rdm[...].astype(F32) + self.rdp[...].astype(F32)


def ring_scratch(count, rows, cols):
    h = rows // 2
    return [
        pltpu.VMEM((count, rows, cols), BF),
        pltpu.VMEM((count, rows, cols), BF),
        pltpu.VMEM((count, rows, cols), BF),
        pltpu.VMEM((count, h, cols), BF),
        pltpu.VMEM((count, h, cols), BF),
        pltpu.VMEM((count, rows, cols), BF),
        pltpu.VMEM((count, rows, cols), BF),
        pltpu.VMEM((count, h, cols), F32),
        pltpu.VMEM((count, h, cols), F32),
    ]


K1_COPIES = 90


def project_kernel(
    act_h, gain_ref, wq_h, wk_h, wv_h, tab_h, out_ref,
    act, scaled, w, tab, sqall, sqr1, sqs, sqr2, sum_a, sum_b, sendq, recvq,
    *rest,
):
    bufs_a, bufs_b, bufs_a2, bufs_b2 = rest[0:9], rest[9:18], rest[18:27], rest[27:36]
    send_sem, recv_sem, local_sem = rest[36:]
    me = Place()
    x, c, y, z = me.x, me.c, me.y, me.z
    net = Net(send_sem, recv_sem)

    own_in = pltpu.make_async_copy(act_h, act.at[0, c], local_sem.at[0])
    own_in.start()
    w_in = [
        pltpu.make_async_copy(wq_h, w.at[:, pl.ds(0, 1024)], local_sem.at[1]),
        pltpu.make_async_copy(wk_h, w.at[:, pl.ds(1024, 128)], local_sem.at[2]),
        pltpu.make_async_copy(wv_h, w.at[:, pl.ds(1152, 128)], local_sem.at[3]),
    ]
    for copy in w_in:
        copy.start()
    tab_in = pltpu.make_async_copy(tab_h, tab.at[me.gy], local_sem.at[4])
    tab_in.start()

    greet(
        [me.at_gy(step) for step in range(1, 8)]
        + [me.at_y(step) for step in range(1, 4)]
        + [me.at_z(step) for step in range(1, 4)]
    )

    top, low = pl.ds(0, 128), pl.ds(128, 128)
    c_sib = net.send(act_h, act.at[0, c], me.sibling)
    c_1a = net.send(act_h.at[top], act.at[3, c, top], me.at_x(1))
    c_2a = net.send(act_h.at[low], act.at[1, c, low], me.at_x(-1))
    c_1b = net.send(act_h.at[low], act.at[3, c, low], me.at_x(1))
    c_2b = net.send(act_h.at[top], act.at[1, c, top], me.at_x(-1))
    c_tab = [net.send(tab_h, tab.at[me.gy], me.at_gy(step)) for step in range(1, 8)]

    gain = gain_ref[...].astype(F32)

    def prep(slot, core):
        for half in range(2):
            wide = act[slot, core, pl.ds(half * 128, 128), :].astype(F32)
            scaled[slot, core, pl.ds(half * 128, 128), :] = (wide * gain).astype(BF)
            square = wide * wide
            fold = (square[:, 0:128] + square[:, 128:256]) + (square[:, 256:384] + square[:, 384:512])
            row = jnp.sum(jnp.transpose(fold), axis=0, keepdims=True)
            sqall[2 * core + half, pl.ds(wrap(x + slot), 1), :] = row

    def rows_of(slot, yy):
        return scaled[slot, lax.div(yy, 2), pl.ds(pl.multiple_of(lax.rem(yy, 2) * 128, 128), 128), :]

    def get_b(slot):
        def get(role):
            return jnp.dot(rows_of(slot, wrap(y + role)), w[:, QA:], preferred_element_type=F32)
        return get

    def get_a(yrole):
        def get(role):
            slot = wrap(z + role - x + 4)
            return jnp.dot(rows_of(slot, wrap(y + yrole)), w[:, :QA], preferred_element_type=F32)
        return get

    ring_b = [RingSum(net, get_b(k), me.at_y(1), me.at_y(-1), bufs_b, k, 128) for k in range(4)]
    ring_a = [RingSum(net, get_a(k), me.at_z(1), me.at_z(-1), bufs_a, k, 128) for k in range(4)]
    ring_a2 = RingSum(net, lambda role: sum_a[role], me.at_y(1), me.at_y(-1), bufs_a2, 0, 128)
    ring_b2 = RingSum(
        net, lambda role: sum_b[wrap(z + role - x + 4)], me.at_z(1), me.at_z(-1), bufs_b2, 0, 128
    )

    own_in.wait()
    prep(0, c)
    for copy in w_in:
        copy.wait()
    c_sib.wait_recv()
    prep(0, 1 - c)
    ring_b[0].start()
    c_1a.wait_recv()
    c_r1 = net.send(act.at[3, c, top], act.at[2, c, top], me.at_x(1))
    c_2a.wait_recv()
    c_r2 = net.send(act.at[1, c, low], act.at[2, c, low], me.at_x(-1))
    ring_b[0].mid()
    c_1b.wait_recv()
    c_s3 = net.send(act.at[3, c], act.at[3, c], me.sibling)
    c_2b.wait_recv()
    c_s1 = net.send(act.at[1, c], act.at[1, c], me.sibling)
    prep(3, c)
    prep(1, c)
    c_s3.wait_recv()
    prep(3, 1 - c)
    ring_b[3].start()
    c_s1.wait_recv()
    prep(1, 1 - c)
    ring_b[1].start()
    sum_b[0] = ring_b[0].finish()
    c_r1.wait_recv()
    c_r2.wait_recv()
    c_s2 = net.send(act.at[2, c], act.at[2, c], me.sibling)
    prep(2, c)
    ring_b[3].mid()
    c_s2.wait_recv()
    prep(2, 1 - c)
    ring_a[2].start()
    ring_b[2].start()
    ring_b[1].mid()
    sq1 = [
        net.send(sqall.at[wrap(y + step)], sqr1.at[step - 1], me.at_y(step)) for step in range(1, 4)
    ]
    ring_a[1].start()
    sum_b[3] = ring_b[3].finish()
    ring_a[2].mid()
    ring_a[3].start()
    ring_b[2].mid()
    sum_b[1] = ring_b[1].finish()
    ring_a[0].start()
    ring_a[1].mid()
    sum_a[2] = ring_a[2].finish()
    for copy in sq1:
        copy.wait_recv()
    sqs[...] = (sqall[y] + sqr1[0]) + (sqr1[1] + sqr1[2])
    sq2 = [net.send(sqs, sqr2.at[step - 1], me.at_z(step)) for step in range(1, 4)]
    ring_a[3].mid()
    sum_b[2] = ring_b[2].finish()
    ring_b2.start()
    sum_a[1] = ring_a[1].finish()
    ring_a[0].mid()
    sum_a[3] = ring_a[3].finish()
    ring_a2.start()
    for copy in sq2:
        copy.wait_recv()
    totals = (sqs[...] + sqr2[0]) + (sqr2[1] + sqr2[2])
    sqs2 = sqr1.at[0]
    sqs2[...] = totals
    own_sq = sqs2[pl.ds(z, 1), :]
    inverse = jnp.transpose(jnp.broadcast_to(lax.rsqrt(own_sq / D + 1e-05), (128, 128)))
    tab_in.wait()
    for copy in c_tab:
        copy.wait_recv()
    both = tab[...].reshape(128, 128)
    turned = pltpu.roll(both, 64, 1)
    first = lax.broadcasted_iota(jnp.int32, (128, 128), 1) < 64
    cosine = jnp.where(first, both, turned)
    sine = jnp.where(first, -turned, both)
    sum_a[0] = ring_a[0].finish()
    ring_b2.mid()
    ring_a2.mid()

    def put(col, block):
        sendq[:, :, pl.ds(col, 128)] = block.astype(BF).reshape(8, 16, 128)

    def rotated(part):
        part = part * inverse
        return part * cosine + pltpu.roll(part, 64, 1) * sine

    fin = ring_b2.finish()
    for head in range(4):
        put(512 + head * 128, rotated(fin[:, head * 128 : (head + 1) * 128]))
    put(1024, rotated(fin[:, 512:640]))
    put(1152, fin[:, 640:768] * inverse)
    fin = ring_a2.finish()
    for head in range(4):
        put(head * 128, rotated(fin[:, head * 128 : (head + 1) * 128]))
    sends = [
        net.send(sendq.at[wrap(me.gy + step, 8)], recvq.at[me.gy], me.at_gy(step))
        for step in range(1, 8)
    ]
    recvq[me.gy] = sendq[me.gy]
    for copy in sends:
        copy.wait_recv()
    out_ref[...] = recvq[...]
    net.drain()
    assert len(net.made) == K1_COPIES


def project(act, gain, wq, wk, wv, tab):
    hbm = pl.BlockSpec(memory_space=pl.ANY)
    vmem = pl.BlockSpec(memory_space=pltpu.VMEM)
    return pl.pallas_call(
        project_kernel,
        out_shape=jax.ShapeDtypeStruct((8, DRAFT, 1280), BF),
        in_specs=[hbm, vmem, hbm, hbm, hbm, hbm],
        out_specs=vmem,
        scratch_shapes=[
            pltpu.VMEM((4, 2, 256, 512), BF),
            pltpu.VMEM((4, 2, 256, 512), BF),
            pltpu.VMEM((512, 1280), BF),
            pltpu.VMEM((8, 16, 128), F32),
            pltpu.VMEM((4, 8, 128), F32),
            pltpu.VMEM((3, 8, 128), F32),
            pltpu.VMEM((8, 128), F32),
            pltpu.VMEM((3, 8, 128), F32),
            pltpu.VMEM((4, 128, QA), F32),
            pltpu.VMEM((4, 128, QB), F32),
            pltpu.VMEM((8, 16, 1280), BF),
            pltpu.VMEM((8, 16, 1280), BF),
            *ring_scratch(4, 128, QA),
            *ring_scratch(4, 128, QB),
            *ring_scratch(1, 128, QA),
            *ring_scratch(1, 128, QB),
            pltpu.SemaphoreType.DMA((K1_COPIES,)),
            pltpu.SemaphoreType.DMA((K1_COPIES,)),
            pltpu.SemaphoreType.DMA((5,)),
        ],
        compiler_params=pltpu.CompilerParams(
            collective_id=0, has_side_effects=True, vmem_limit_bytes=56 * 1024 * 1024
        ),
        name="project",
    )(act, gain, wq, wk, wv, tab)


LOG2E = 1.4426950408889634


def attend_kernel(len_ref, qkv_ref, k_ref, v_ref, out_ref):
    packed = qkv_ref[0]
    query = jnp.concatenate([packed[:, h * 128 : (h + 1) * 128] for h in range(8)], axis=0)
    fresh_key, fresh_value = packed[:, 1024:1152], packed[:, 1152:1280]
    scale = HD ** (-0.5) * LOG2E
    contract = (((1,), (1,)), ((), ()))
    old = lax.dot_general(query, k_ref[0], contract, preferred_element_type=F32) * scale
    new = lax.dot_general(query, fresh_key, contract, preferred_element_type=F32) * scale
    old = jnp.where(lax.broadcasted_iota(jnp.int32, (1, CTX), 1) < len_ref[0], old, -1e30)
    token = lax.rem(lax.broadcasted_iota(jnp.int32, (128, 16), 0), 16)
    causal = lax.broadcasted_iota(jnp.int32, (128, 16), 1) <= token
    new = jnp.where(causal, new, -1e30)
    highest = jnp.maximum(
        jnp.max(old, axis=1, keepdims=True), jnp.max(new, axis=1, keepdims=True)
    )
    old = jnp.exp2(old - highest)
    new = jnp.exp2(new - highest)
    total = jnp.sum(old, axis=1, keepdims=True) + jnp.sum(new, axis=1, keepdims=True)
    blend = jnp.dot(old.astype(BF), v_ref[0], preferred_element_type=F32)
    blend = blend + jnp.dot(new.astype(BF), fresh_value, preferred_element_type=F32)
    result = (blend / total).astype(BF)
    out_ref[0] = jnp.concatenate([result[h * 16 : (h + 1) * 16] for h in range(8)], axis=1)


def attend(lengths, qkv, key_cache, value_cache):
    return pl.pallas_call(
        attend_kernel,
        out_shape=jax.ShapeDtypeStruct((8, DRAFT, 1024), BF),
        grid=(8,),
        in_specs=[
            pl.BlockSpec(memory_space=pltpu.SMEM),
            pl.BlockSpec((1, DRAFT, 1280), lambda g: (g, 0, 0)),
            pl.BlockSpec((1, CTX, 128), lambda g: (0, 0, g)),
            pl.BlockSpec((1, CTX, 128), lambda g: (0, 0, g)),
        ],
        out_specs=pl.BlockSpec((1, DRAFT, 1024), lambda g: (g, 0, 0)),
        compiler_params=pltpu.CompilerParams(vmem_limit_bytes=56 * 1024 * 1024),
        name="attend",
    )(lengths, qkv, key_cache, value_cache)


def places_table(position):
    frequency = jnp.exp(
        jnp.arange(64, dtype=F32) * (-2.0 * math.log(500000.0) / HD)
    )
    places = position + jnp.arange(DRAFT, dtype=jnp.int32)
    angles = places.astype(F32)[:, None] * frequency
    return jnp.concatenate([jnp.cos(angles), jnp.sin(angles)], axis=-1)


def shards(act, gain, wq, wk, wv, wo, key_cache, value_cache, lengths, positions):
    act = act.reshape(256, 512)
    qkv = project(act, gain.reshape(1, 512), wq, wk, wv, places_table(positions))
    attended = attend(lengths, qkv, key_cache, value_cache)
    regrouped = lax.all_to_all(attended, "gy", split_axis=0, concat_axis=0, tiled=True)
    gathered = lax.all_gather(regrouped, "gx", axis=0, tiled=True)
    terms = jnp.einsum("btf,fd->btd", gathered, wo, preferred_element_type=F32)
    return lax.psum_scatter(terms.astype(BF), "gy", scatter_dimension=0, tiled=True)


def solution(mesh):
    return jax.shard_map(
        shards,
        mesh=mesh,
        in_specs=(
            P("gy", None, "gx"),
            P("gx"),
            P("gx", "gy"),
            P("gx", "gy"),
            P("gx", "gy"),
            P("gy", "gx"),
            P(("gx", "gy"), None, None),
            P(("gx", "gy"), None, None),
            P(("gx", "gy")),
            P(("gx", "gy")),
        ),
        out_specs=P("gy", None, "gx"),
        check_vma=False,
    )
```

time: 518 us -> 199 us (0.38)
  waiting for transfers between devices: 252 us -> 78.6 us
  Pallas kernels: 0 us -> 79.3 us
  blocking collectives: 78.4 us -> 10.8 us
  other arithmetic: 59.9 us -> 0.8 us
  local copies, waits for them, and re-layouts: 47 us -> 3.08 us
  matrix products: 47.5 us -> 8.86 us
  starting transfers between devices: 15.4 us -> 0.22 us
    reduce_scatter x4 -> x1, waiting for transfers between devices: 166 us -> 30.4 us  [shards(): lax.psum_scatter(terms.astype(BF), 'gy', scatter_dimension=0, tiled=True)]
    pallas_call x0 -> x2, Pallas kernels: none -> 79.3 us  [the longest x1 65.5 us: project(): pl.pallas_call(project_kernel, out_shape=jax.ShapeDtypeStruct((8, DRAFT,...]
    psum x1 -> x0, blocking collectives: 60.8 us -> none  [shards(): totals = lax.psum(squares, 'gx')]
    unnamed x1 -> x0, other arithmetic: 45.2 us -> none
    dot_general x8 -> x1, matrix products: 47.5 us -> 8.86 us  [shards(): terms = jnp.einsum('btf,fd->btd', gathered, wo, preferred_element_type=F32)]
    all_gather x2 -> x1, waiting for transfers between devices: 79.5 us -> 48.2 us  [shards(): gathered = lax.all_gather(regrouped, 'gx', axis=0, tiled=True)]
    unnamed x18 -> x2, local copies, waits for them, and re-layouts: 26.9 us -> 0.01 us
    all_to_all x3 -> x0, starting transfers between devices: 15.2 us -> none  [the longest x1 6.11 us: shards(): lax.all_to_all(query_rot, 'gy', split_axis=0, concat_axis=2, tiled=True)]
  transfers between devices with their start and end apart: 9 -> 2, of which waited for: 6 -> 2; matrix products, arithmetic and copies ran while one was open for 13% -> 0% of each run, Pallas kernels for 0% -> 0%
where the time goes in v1:
time: 199 us; the launch traced here: 196 us
  Pallas kernels  79.3 us (40%)
  waiting for transfers between devices  78.6 us (39%)
  between operations  14.8 us (7%)
  blocking collectives  10.8 us (5%)
  matrix products  8.86 us (4%)
  local copies, waits for them, and re-layouts  3.08 us (2%)
    pallas_call x1, Pallas kernels, project(): pl.pallas_call(project_kernel, out_shape=jax.ShapeDtypeStruct((8, DRAFT,...  65.5 us
    all_gather x1, waiting for transfers between devices, shards(): gathered = lax.all_gather(regrouped, 'gx', axis=0, tiled=True)  48.2 us
    reduce_scatter x1, waiting for transfers between devices, shards(): lax.psum_scatter(terms.astype(BF), 'gy', scatter_dimension=0, tiled=True)  30.4 us
    pallas_call x1, Pallas kernels, attend(): pl.pallas_call(attend_kernel, out_shape=jax.ShapeDtypeStruct((8, DRAFT, 1...  13.8 us
    all_to_all x1, blocking collectives, shards(): lax.all_to_all(attended, 'gy', split_axis=0, concat_axis=0, tiled=True)  10.8 us
    dot_general x1, matrix products, shards(): terms = jnp.einsum('btf,fd->btd', gathered, wo, preferred_element_type=F32)  8.86 us
  transfers between devices with their start and end apart: 2, of which 2 were waited for; matrix products, arithmetic and copies ran while one was open for 0% of the time, Pallas kernels for 0%

profile of v1, /device:TPU:1, one launch (start us, length us, event | category | flops | bytes accessed | tf_op | source)
XLA Modules:
  0.0 196.5 jit_solution(14561031654231070053)
XLA Ops:
  6.5 0.0 copy-start
  6.5 0.0 all-gather.2.cloned.1.call-start
  8.0 1.3 reshape.17.gain_ref
  9.2 0.1 multiply_cosine_fusion
  9.3 0.7 pad_maximum_fusion.tab_h
  10.0 65.5 %project.1.qkv_ref = bf16[8,16,1280]{2,1,0:T(8,128)(2,1)} custom-call(bf16[256,512]{1,0:T(8,128)(2,1)} %bitcast.6, bf16[1,512]{1,0:T(2,128)(2,1)} %reshape.17.gain_ref, bf16[512,1024]{1,0:T(8,128)(2,1)} %wq_h.1, bf16[512,128]{1,0:T(8,128)(2,1)} %wk_h.1, bf16[512,128]{1,0:T(8,128)(2,1)} %wv_h.1, f32[16,128]{1,0:T(8,128)} %pad_maximum_fusion.tab_h), custom_call_target="tpu_custom_call" | custom-call | tf_op jit(solution)/shard_map/project/pallas_call | solution.py:312
  75.5 13.8 %attend.1 = bf16[8,16,1024]{2,1,0:T(8,128)(2,1)} custom-call(s32[1]{0:T(128)S(6)} %copy.19.len_ref, bf16[8,16,1280]{2,1,0:T(8,128)(2,1)} %project.1.qkv_ref, bf16[1,4096,1024]{2,1,0:T(8,128)(2,1)} %k_ref.1, bf16[1,4096,1024]{2,1,0:T(8,128)(2,1)} %v_ref.1), custom_call_target="tpu_custom_call" | custom-call | tf_op jit(solution)/shard_map/attend/pallas_call | solution.py:373
  89.3 10.8 %all_to_all.5 = bf16[8,16,1024]{2,1,0:T(8,128)(2,1)} all-to-all(bf16[8,16,1024]{2,1,0:T(8,128)(2,1)} %attend.1), channel_id=1, replica_groups=mesh['gx'=16,'gy'=8] {'gy'}, dimensions={0} | all-to-all | bytes 524288 | tf_op jit(solution)/shard_map/all_to_all | solution.py:402
  100.1 0.0 all-gather.2.cloned.1.call-update
  100.1 0.2 reduce-scatter.2.cloned.1.call-start
  100.4 48.2 %all-gather.2.cloned.1.call-done = bf16[128,16,1024]{2,1,0:T(8,128)(2,1)} async-done(((bf16[8,16,1024]{2,1,0:T(8,128)(2,1)}), bf16[128,16,1024]{2,1,0:T(8,128)(2,1)}) %all-gather.2.cloned.1.call-update) | async-done | bytes 4194320 | tf_op jit(solution)/shard_map/all_gather | solution.py:403
  148.6 0.0 copy-done
  148.6 8.9 %fusion.2 = bf16[128,16,512]{2,0,1:T(8,128)(2,1)} fusion(bf16[128,16,1024]{2,1,0:T(8,128)(2,1)} %all-gather.2.cloned.1.call-done, bf16[1024,512]{1,0:T(8,128)(2,1)S(1)} %copy-done), kind=kOutput, calls=%fused_computation.2 | convolution fusion | flops 2148532224 | bytes 7340032 | tf_op jit(solution)/shard_map/btf,fd->btd/dot_general | solution.py:404
  157.4 0.0 reduce-scatter.2.cloned.1.call-update
  157.4 30.4 %reduce-scatter.2.cloned.1.call-done = bf16[16,16,512]{2,0,1:T(8,128)(2,1)} async-done(((bf16[128,16,512]{2,0,1:T(8,128)(2,1)}), bf16[16,16,512]{2,0,1:T(8,128)(2,1)}) %reduce-scatter.2.cloned.1.call-update) | async-done | bytes 262160 | tf_op jit(solution)/shard_map/reduce_scatter | solution.py:405
  187.9 1.8 copy.14
  (2 shorter events, 0.0 us)
Async XLA Ops:
  6.5 142.0 %copy-start = (bf16[1024,512]{1,0:T(8,128)(2,1)S(1)}, bf16[1024,512]{1,0:T(8,128)(2,1)}, u32[]{:S(2)}) copy-start(bf16[1024,512]{1,0:T(8,128)(2,1)} %param.15) | copy-start | bytes 3145732
  6.5 142.0 %all-gather.2.cloned.1.call-start = ((), (), s32[]{:S(2)}) async-start(), calls=%async_computation.2 | async-start | bytes 4456448 | tf_op jit(solution)/shard_map/all_gather | solution.py:403
  100.1 87.7 %reduce-scatter.2.cloned.1.call-start = ((), (), s32[]{:S(2)}) async-start(), calls=%async_computation.3 | async-start | bytes 2359296 | tf_op jit(solution)/shard_map/reduce_scatter | solution.py:405
Sparse Core Ops, SparseCore 0:
  100.2 48.2 all-gather.1
  157.6 30.2 reduce-scatter.1

commit v2 on v1

--- a/solution.py
+++ b/solution.py
@@ -386,6 +386,173 @@
     )(lengths, qkv, key_cache, value_cache)
 
 
+class RingCast:
+    def __init__(self, net, slots, plus, minus):
+        self.net, self.slots, self.plus, self.minus = net, slots, plus, minus
+        self.lo, self.hi = pl.ds(0, 32), pl.ds(32, 32)
+
+    def start(self):
+        net, lo, hi = self.net, self.lo, self.hi
+        own, next_, _, last = self.slots
+        self.c_pl = net.send(own.at[lo], last.at[lo], self.plus)
+        self.c_mh = net.send(own.at[hi], next_.at[hi], self.minus)
+        self.c_ph = net.send(own.at[hi], last.at[hi], self.plus)
+        self.c_ml = net.send(own.at[lo], next_.at[lo], self.minus)
+
+    def relay(self):
+        net, lo, hi = self.net, self.lo, self.hi
+        _, next_, far, last = self.slots
+        self.c_pl.wait_recv()
+        self.c_rp = net.send(last.at[lo], far.at[lo], self.plus)
+        self.c_mh.wait_recv()
+        self.c_rm = net.send(next_.at[hi], far.at[hi], self.minus)
+
+    def near(self):
+        self.c_ph.wait_recv()
+        self.c_ml.wait_recv()
+
+    def far(self):
+        self.c_rp.wait_recv()
+        self.c_rm.wait_recv()
+
+
+K3_COPIES = 77
+
+
+def out_kernel(att_h, wo_h, out_ref, g, wo, part, sib_send, sib_recv, *rest):
+    bufs = rest[0:9]
+    send_sem, recv_sem, local_sem = rest[9:]
+    me = Place()
+    x, c, y, z = me.x, me.c, me.y, me.z
+    net = Net(send_sem, recv_sem)
+    w_in = pltpu.make_async_copy(wo_h, wo, local_sem.at[0])
+    w_in.start()
+    spot = pl.ds(pl.multiple_of(lax.rem(me.gy, 4) * 16, 16), 16)
+    own_in = pltpu.make_async_copy(
+        att_h.at[me.gy], g.at[lax.div(me.gy, 4), 0, 0, spot], local_sem.at[1]
+    )
+    own_in.start()
+    greet(
+        [me.at_gy(step) for step in range(1, 8)]
+        + [me.at_y(1), me.at_y(-1), me.at_z(1), me.at_z(-1)]
+    )
+    swap = [
+        net.send(
+            att_h.at[wrap(me.gy + step, 8)], g.at[lax.div(me.gy, 4), 0, 0, spot], me.at_gy(step)
+        )
+        for step in range(1, 8)
+    ]
+    ym, yp, zm, zp = me.at_y(-1), me.at_y(1), me.at_z(-1), me.at_z(1)
+    a1 = RingCast(net, [g.at[0, k, 0] for k in range(4)], zp, zm)
+    b1 = RingCast(net, [g.at[1, 0, k] for k in range(4)], yp, ym)
+    a2 = [RingCast(net, [g.at[0, j, k] for k in range(4)], yp, ym) for j in range(4)]
+    b2 = [RingCast(net, [g.at[1, k, j] for k in range(4)], zp, zm) for j in range(4)]
+    own_in.wait()
+    for copy in swap:
+        copy.wait_recv()
+    a1.start()
+    b1.start()
+    a2[0].start()
+    b2[0].start()
+    a1.relay()
+    b1.relay()
+    a1.near()
+    a2[1].start()
+    a2[3].start()
+    b1.near()
+    b2[1].start()
+    b2[3].start()
+    a2[0].relay()
+    b2[0].relay()
+    a1.far()
+    a2[2].start()
+    b1.far()
+    b2[2].start()
+    a2[1].relay()
+    b2[1].relay()
+    a2[3].relay()
+    b2[3].relay()
+    w_in.wait()
+    pair = [None] * 4
+
+    def multiply(dz):
+        for mine in (False, True):
+            core = c if mine else 1 - c
+            for half in range(2):
+                rows = jnp.concatenate(
+                    [g[half, dz, wrap(core * 2 + i - y)] for i in range(2)], axis=0
+                )
+                term = jnp.dot(rows, wo[...], preferred_element_type=F32)
+                if mine:
+                    part[dz, pl.ds(half * 128, 128), :] = term
+                else:
+                    sib_send[dz, pl.ds(half * 128, 128), :] = term.astype(BF)
+            if not mine:
+                pair[dz] = net.send(sib_send.at[dz], sib_recv.at[dz], me.sibling)
+
+    a2[0].near()
+    a2[0].far()
+    multiply(0)
+    a2[2].relay()
+    b2[2].relay()
+    for ring in a2[1], a2[3]:
+        ring.near()
+        ring.far()
+    for ring in b2:
+        ring.near()
+    multiply(1)
+    multiply(3)
+    a2[2].near()
+    a2[2].far()
+    for ring in b2:
+        ring.far()
+    multiply(2)
+    for copy in pair:
+        copy.wait_recv()
+
+    def get(role):
+        dz = wrap(x + role - z + 4)
+        return part[dz] + sib_recv[dz].astype(F32)
+
+    ring = RingSum(net, get, me.at_x(1), me.at_x(-1), bufs, 0, 256)
+    ring.start()
+    ring.mid()
+    done = ring.finish().astype(BF)
+    for half in range(2):
+        for i in range(2):
+            out_ref[pl.ds(i * 128 + half * 64, 64), :] = done[
+                half * 128 + i * 64 : half * 128 + i * 64 + 64
+            ]
+    net.drain()
+    assert len(net.made) == K3_COPIES
+
+
+def project_out(att, wo):
+    hbm = pl.BlockSpec(memory_space=pl.ANY)
+    vmem = pl.BlockSpec(memory_space=pltpu.VMEM)
+    return pl.pallas_call(
+        out_kernel,
+        out_shape=jax.ShapeDtypeStruct((256, 512), BF),
+        in_specs=[hbm, hbm],
+        out_specs=vmem,
+        scratch_shapes=[
+            pltpu.VMEM((2, 4, 4, 64, 1024), BF),
+            pltpu.VMEM((1024, 512), BF),
+            pltpu.VMEM((4, 256, 512), F32),
+            pltpu.VMEM((4, 256, 512), BF),
+            pltpu.VMEM((4, 256, 512), BF),
+            *ring_scratch(1, 256, 512),
+            pltpu.SemaphoreType.DMA((K3_COPIES,)),
+            pltpu.SemaphoreType.DMA((K3_COPIES,)),
+            pltpu.SemaphoreType.DMA((2,)),
+        ],
+        compiler_params=pltpu.CompilerParams(
+            collective_id=1, has_side_effects=True, vmem_limit_bytes=56 * 1024 * 1024
+        ),
+        name="project_out",
+    )(att, wo)
+
+
 def places_table(position):
     frequency = jnp.exp(
         jnp.arange(64, dtype=F32) * (-2.0 * math.log(500000.0) / HD)
@@ -399,10 +566,7 @@
     act = act.reshape(256, 512)
     qkv = project(act, gain.reshape(1, 512), wq, wk, wv, places_table(positions))
     attended = attend(lengths, qkv, key_cache, value_cache)
-    regrouped = lax.all_to_all(attended, "gy", split_axis=0, concat_axis=0, tiled=True)
-    gathered = lax.all_gather(regrouped, "gx", axis=0, tiled=True)
-    terms = jnp.einsum("btf,fd->btd", gathered, wo, preferred_element_type=F32)
-    return lax.psum_scatter(terms.astype(BF), "gy", scatter_dimension=0, tiled=True)
+    return project_out(attended, wo).reshape(16, DRAFT, 512)
 
 
 def solution(mesh):

time: 199 us -> 131 us (0.66)
  waiting for transfers between devices: 78.6 us -> 0 us
  Pallas kernels: 79.3 us -> 125 us
  between operations: 14.8 us -> 1.33 us
  blocking collectives: 10.8 us -> 0 us
  matrix products: 8.86 us -> 0 us
    all_gather x1 -> x0, waiting for transfers between devices: 48.2 us -> none  [shards(): gathered = lax.all_gather(regrouped, 'gx', axis=0, tiled=True)]
    pallas_call x0 -> x1, Pallas kernels: none -> 45.6 us  [project_out(): pl.pallas_call(out_kernel, out_shape=jax.ShapeDtypeStruct((256, 512), BF)...]
    reduce_scatter x1 -> x0, waiting for transfers between devices: 30.4 us -> none  [shards(): lax.psum_scatter(terms.astype(BF), 'gy', scatter_dimension=0, tiled=True)]
    all_to_all x1 -> x0, blocking collectives: 10.8 us -> none  [shards(): lax.all_to_all(attended, 'gy', split_axis=0, concat_axis=0, tiled=True)]
    dot_general x1 -> x0, matrix products: 8.86 us -> none  [shards(): terms = jnp.einsum('btf,fd->btd', gathered, wo, preferred_element_type=F32)]
  transfers between devices with their start and end apart: 2 -> 0, of which waited for: 2 -> 0; matrix products, arithmetic and copies ran while one was open for 0% -> 0% of each run, Pallas kernels for 0% -> 0%
where the time goes in v2:
time: 131 us; the launch traced here: 130 us
  Pallas kernels  125 us (95%)
  local copies, waits for them, and re-layouts  2.94 us (2%)
  between operations  1.33 us (1%)
    pallas_call x1, Pallas kernels, project(): pl.pallas_call(project_kernel, out_shape=jax.ShapeDtypeStruct((8, DRAFT,...  65.5 us
    pallas_call x1, Pallas kernels, project_out(): pl.pallas_call(out_kernel, out_shape=jax.ShapeDtypeStruct((256, 512), BF)...  45.6 us
    pallas_call x1, Pallas kernels, attend(): pl.pallas_call(attend_kernel, out_shape=jax.ShapeDtypeStruct((8, DRAFT, 1...  14 us

profile of v2, /device:TPU:1, one launch (start us, length us, event | category | flops | bytes accessed | tf_op | source)
XLA Modules:
  0.0 130.1 jit_solution(14790525115031442616)
XLA Ops:
  1.3 1.3 reshape.20.gain_ref
  2.6 0.1 multiply_cosine_fusion
  2.7 0.7 pad_maximum_fusion.tab_h
  3.4 65.5 %project.1.qkv_ref = bf16[8,16,1280]{2,1,0:T(8,128)(2,1)} custom-call(bf16[256,512]{1,0:T(8,128)(2,1)} %bitcast.5, bf16[1,512]{1,0:T(2,128)(2,1)} %reshape.20.gain_ref, bf16[512,1024]{1,0:T(8,128)(2,1)} %wq_h.1, bf16[512,128]{1,0:T(8,128)(2,1)} %wk_h.1, bf16[512,128]{1,0:T(8,128)(2,1)} %wv_h.1, f32[16,128]{1,0:T(8,128)} %pad_maximum_fusion.tab_h), custom_call_target="tpu_custom_call" | custom-call | tf_op jit(solution)/shard_map/project/pallas_call | solution.py:312
  68.9 14.0 %attend.1.att_h = bf16[8,16,1024]{2,1,0:T(8,128)(2,1)} custom-call(s32[1]{0:T(128)S(6)} %copy.12.len_ref, bf16[8,16,1280]{2,1,0:T(8,128)(2,1)} %project.1.qkv_ref, bf16[1,4096,1024]{2,1,0:T(8,128)(2,1)} %k_ref.1, bf16[1,4096,1024]{2,1,0:T(8,128)(2,1)} %v_ref.1), custom_call_target="tpu_custom_call" | custom-call | tf_op jit(solution)/shard_map/attend/pallas_call | solution.py:373
  82.9 45.6 %project_out.1 = bf16[256,512]{1,0:T(8,128)(2,1)} custom-call(bf16[8,16,1024]{2,1,0:T(8,128)(2,1)} %attend.1.att_h, bf16[1024,512]{1,0:T(8,128)(2,1)} %wo_h.1), custom_call_target="tpu_custom_call" | custom-call | tf_op jit(solution)/shard_map/project_out/pallas_call | solution.py:533
  128.5 1.7 %copy.14 = bf16[16,16,512]{2,1,0:T(8,128)(2,1)} copy(bf16[16,16,512]{2,1,0:T(8,128)(2,1)} %bitcast.4) | data formatting | bytes 524288
  (2 shorter events, 0.0 us)

commit v3 on v1

v3 whole, which is shorter than its diff:
```python
import math

import jax
import jax.numpy as jnp
from jax import lax
from jax.experimental import pallas as pl
from jax.experimental.pallas import tpu as pltpu
from jax.sharding import PartitionSpec as P

D = 8192
HD = 128
KV = 8
CTX = 4096
DRAFT = 16
MESH = pl.DeviceIdType.MESH
F32 = jnp.float32
BF = jnp.bfloat16


def wrap(value, size=4):
    return lax.rem(value + size, size)


class Place:
    def __init__(self):
        gx, gy = lax.axis_index("gx"), lax.axis_index("gy")
        self.gx, self.gy = gx, gy
        self.z, self.y = lax.div(gx, 4), lax.rem(gx, 4)
        self.x, self.c = lax.div(gy, 2), lax.rem(gy, 2)
        self.sibling = (gx, gy + 1 - 2 * self.c)

    def at_x(self, step):
        return (self.gx, wrap(self.x + step) * 2 + self.c)

    def at_y(self, step):
        return (self.z * 4 + wrap(self.y + step), self.gy)

    def at_z(self, step):
        return (wrap(self.z + step) * 4 + self.y, self.gy)

    def at_gy(self, step):
        return (self.gx, wrap(self.gy + step, 8))


class Net:
    def __init__(self, send_sem, recv_sem):
        self.send_sem, self.recv_sem = send_sem, recv_sem
        self.count = 0
        self.sent = []

    def make(self, src, dst, device, drained=True):
        copy = pltpu.make_async_remote_copy(
            src_ref=src,
            dst_ref=dst,
            send_sem=self.send_sem.at[self.count],
            recv_sem=self.recv_sem.at[self.count],
            device_id=device,
            device_id_type=MESH,
        )
        self.count += 1
        if drained:
            self.sent.append(copy)
        return copy

    def send(self, src, dst, device):
        copy = self.make(src, dst, device)
        copy.start()
        return copy

    def drain(self):
        for copy in self.sent:
            copy.wait_send()


def greet(devices):
    barrier = pltpu.get_barrier_semaphore()
    for device in devices:
        pl.semaphore_signal(barrier, inc=1, device_id=device, device_id_type=MESH)
    pl.semaphore_wait(barrier, len(devices))


class RingSum:
    def __init__(self, net, get, plus, minus, bufs, lead, rows, drained=True):
        self.get = get
        self.rows, self.half = rows, rows // 2
        self.so, self.sp, self.sm, self.rom, self.rop, self.rdm, self.rdp, self.kp, self.km = [
            buf.at[lead] for buf in bufs
        ]
        lo, hi = pl.ds(0, self.half), pl.ds(self.half, self.half)
        self.lo, self.hi = lo, hi
        self.om = net.make(self.so.at[lo], self.rom, plus, drained)
        self.op = net.make(self.so.at[hi], self.rop, minus, drained)
        self.m1 = net.make(self.sp.at[hi], self.rdm.at[hi], plus, drained)
        self.p1 = net.make(self.sm.at[lo], self.rdp.at[lo], minus, drained)
        self.m2 = net.make(self.sp.at[lo], self.rdm.at[lo], plus, drained)
        self.p2 = net.make(self.sm.at[hi], self.rdp.at[hi], minus, drained)
        self.copies = [self.om, self.op, self.m1, self.p1, self.m2, self.p2]

    def start(self):
        h = self.half
        self.so[...] = self.get(2).astype(BF)
        self.om.start()
        self.op.start()
        part = self.get(1)
        self.kp[...] = part[:h]
        self.sp[self.hi] = part[h:].astype(BF)
        self.m1.start()
        part = self.get(3)
        self.km[...] = part[h:]
        self.sm[self.lo] = part[:h].astype(BF)
        self.p1.start()

    def mid(self):
        self.om.wait_recv()
        self.sp[self.lo] = (self.kp[...] + self.rom[...].astype(F32)).astype(BF)
        self.m2.start()
        self.op.wait_recv()
        self.sm[self.hi] = (self.km[...] + self.rop[...].astype(F32)).astype(BF)
        self.p2.start()

    def finish(self):
        own = self.get(0)
        for copy in (self.m1, self.p1, self.m2, self.p2):
            copy.wait_recv()
        return own + self.rdm[...].astype(F32) + self.rdp[...].astype(F32)


def ring_scratch(count, rows, cols):
    h = rows // 2
    return [
        pltpu.VMEM((count, rows, cols), BF),
        pltpu.VMEM((count, rows, cols), BF),
        pltpu.VMEM((count, rows, cols), BF),
        pltpu.VMEM((count, h, cols), BF),
        pltpu.VMEM((count, h, cols), BF),
        pltpu.VMEM((count, rows, cols), BF),
        pltpu.VMEM((count, rows, cols), BF),
        pltpu.VMEM((count, h, cols), F32),
        pltpu.VMEM((count, h, cols), F32),
    ]


class BlockSum:
    def __init__(self, net, role, slot, plus, minus, bufs, parts, rows):
        self.role, self.slot, self.parts = role, slot, parts
        self.out, self.rom, self.rop, self.rdm, self.rdp, self.keep = bufs
        h = rows // 2
        lo, hi = pl.ds(0, h), pl.ds(h, h)
        self.lo, self.hi = lo, hi
        far, near, last = slot(2), slot(1), slot(3)
        span = range(parts)
        self.om = [net.make(self.out.at[far, j, lo], self.rom.at[j], plus) for j in span]
        self.op = [net.make(self.out.at[far, j, hi], self.rop.at[j], minus) for j in span]
        self.m1 = [net.make(self.out.at[near, j, hi], self.rdm.at[j, hi], plus) for j in span]
        self.p1 = [net.make(self.out.at[last, j, lo], self.rdp.at[j, lo], minus) for j in span]
        self.m2 = [net.make(self.out.at[near, j, lo], self.rdm.at[j, lo], plus) for j in span]
        self.p2 = [net.make(self.out.at[last, j, hi], self.rdp.at[j, hi], minus) for j in span]

    def block(self, k, get):
        role = self.role(k)
        for j in (2, 1, 3, 0)[-self.parts :] if self.parts == 4 else range(self.parts):
            value = get(j)
            self.out[k, j] = value.astype(BF)
            if self.keep is not None:
                self.keep[k, j] = value

            @pl.when(role == 2)
            def _():
                self.om[j].start()
                self.op[j].start()

            @pl.when(role == 1)
            def _():
                self.m1[j].start()

            @pl.when(role == 3)
            def _():
                self.p1[j].start()

    def value(self, k, j, rows):
        if self.keep is not None:
            return self.keep[k, j, rows]
        return self.out[k, j, rows].astype(F32)

    def mid(self, k):
        role = self.role(k)
        order = (2, 1, 3, 0) if self.parts == 4 else range(self.parts)

        @pl.when(role == 1)
        def _():
            for j in order:
                self.om[j].wait_recv()
                total = self.value(k, j, self.lo) + self.rom[j].astype(F32)
                self.out[k, j, self.lo] = total.astype(BF)
                self.m2[j].start()

        @pl.when(role == 3)
        def _():
            for j in order:
                self.op[j].wait_recv()
                total = self.value(k, j, self.hi) + self.rop[j].astype(F32)
                self.out[k, j, self.hi] = total.astype(BF)
                self.p2[j].start()

    def finish(self, j):
        own = self.value(self.slot(0), j, slice(None))
        for copy in (self.m1[j], self.p1[j], self.m2[j], self.p2[j]):
            copy.wait_recv()
        return own + self.rdm[j].astype(F32) + self.rdp[j].astype(F32)


def block_scratch(parts, rows, cols):
    return [
        pltpu.VMEM((4, parts, rows, cols), BF),
        pltpu.VMEM((parts, rows // 2, cols), BF),
        pltpu.VMEM((parts, rows // 2, cols), BF),
        pltpu.VMEM((parts, rows, cols), BF),
        pltpu.VMEM((parts, rows, cols), BF),
    ]


class RingCast:
    def __init__(self, net, slots, plus, minus):
        lo, hi = pl.ds(0, 32), pl.ds(32, 32)
        own, next_, far, last = slots
        self.pl = net.make(own.at[lo], last.at[lo], plus)
        self.mh = net.make(own.at[hi], next_.at[hi], minus)
        self.ph = net.make(own.at[hi], last.at[hi], plus)
        self.ml = net.make(own.at[lo], next_.at[lo], minus)
        self.rp = net.make(last.at[lo], far.at[lo], plus)
        self.rm = net.make(next_.at[hi], far.at[hi], minus)

    def start(self):
        for copy in (self.pl, self.mh, self.ph, self.ml):
            copy.start()

    def relay(self):
        self.pl.wait_recv()
        self.rp.start()
        self.mh.wait_recv()
        self.rm.start()

    def near(self):
        self.ph.wait_recv()
        self.ml.wait_recv()

    def far(self):
        self.rp.wait_recv()
        self.rm.wait_recv()


COLS = 640
COPIES = 192
CHUNK = 512


def layer_kernel(
    act_h, gain_ref, wq_h, wk_h, wv_h, wo_h, tab_h, len_ref, k_h, v_h, out_ref,
    act, scaled, w, tab, sqall, sqr1, sqs, sqr2, sendq, recvq, kv, vv, bias, score, att,
    g, wo, sib_send, sib_recv, keep_b, *rest,
):
    bufs_a, rest = rest[:5], rest[5:]
    bufs_b2, rest = rest[:5], rest[5:]
    bufs_b, rest = rest[:9], rest[9:]
    bufs_a2, rest = rest[:9], rest[9:]
    bufs_x, rest = rest[:9], rest[9:]
    send_sem, recv_sem, local_sem = rest
    me = Place()
    x, c, y, z, gy = me.x, me.c, me.y, me.z, me.gy
    net = Net(send_sem, recv_sem)
    ym, yp, zm, zp = me.at_y(-1), me.at_y(1), me.at_z(-1), me.at_z(1)

    local = []

    def fetch(src, dst):
        copy = pltpu.make_async_copy(src, dst, local_sem.at[len(local)])
        copy.start()
        local.append(copy)
        return copy

    own_in = fetch(act_h, act.at[0, c])
    w_in = [
        fetch(wq_h.at[:, pl.ds(0, 512)], w.at[:, pl.ds(0, 512)]),
        fetch(wk_h, w.at[:, pl.ds(512, 128)]),
        fetch(wq_h.at[:, pl.ds(512, 512)], w.at[:, pl.ds(640, 512)]),
        fetch(wv_h, w.at[:, pl.ds(1152, 128)]),
    ]
    tab_in = fetch(tab_h, tab.at[gy])

    greet(
        [me.at_gy(step) for step in range(1, 8)]
        + [me.at_y(step) for step in range(1, 4)]
        + [me.at_z(step) for step in range(1, 4)]
    )

    top, low = pl.ds(0, 128), pl.ds(128, 128)
    c_sib = net.send(act_h, act.at[0, c], me.sibling)
    c_1a = net.send(act_h.at[top], act.at[3, c, top], me.at_x(1))
    c_2a = net.send(act_h.at[low], act.at[1, c, low], me.at_x(-1))
    c_1b = net.send(act_h.at[low], act.at[3, c, low], me.at_x(1))
    c_2b = net.send(act_h.at[top], act.at[1, c, top], me.at_x(-1))
    c_tab = [net.send(tab_h, tab.at[gy], me.at_gy(step)) for step in range(1, 8)]

    gain = gain_ref[...].astype(F32)

    def prep(slot, core):
        for half in range(2):
            wide = act[slot, core, pl.ds(half * 128, 128), :].astype(F32)
            scaled[slot, core, pl.ds(half * 128, 128), :] = (wide * gain).astype(BF)
            square = wide * wide
            fold = (square[:, 0:128] + square[:, 128:256]) + (square[:, 256:384] + square[:, 384:512])
            row = jnp.sum(jnp.transpose(fold), axis=0, keepdims=True)
            sqall[2 * core + half, pl.ds(wrap(x + slot), 1), :] = row

    def rows_of(slot, yy):
        return scaled[slot, lax.div(yy, 2), pl.ds(pl.multiple_of(lax.rem(yy, 2) * 128, 128), 128), :]

    def get_b(slot):
        def get(role):
            return jnp.dot(rows_of(slot, wrap(y + role)), w[:, COLS:], preferred_element_type=F32)
        return get

    def get_a(slot):
        def get(part):
            return jnp.dot(rows_of(slot, wrap(y + part)), w[:, :COLS], preferred_element_type=F32)
        return get

    def role_z(slot):
        return wrap(x + slot - z + 4)

    def slot_z(role):
        return wrap(z + role - x + 4)

    ring_b = [RingSum(net, get_b(k), yp, ym, bufs_b, k, 128) for k in range(4)]
    sum_a = BlockSum(net, role_z, slot_z, zp, zm, (*bufs_a, None), 4, 128)
    sum_b = BlockSum(net, role_z, slot_z, zp, zm, (*bufs_b2, keep_b), 1, 128)
    ring_a2 = RingSum(net, sum_a.finish, yp, ym, bufs_a2, 0, 128)

    own_in.wait()
    prep(0, c)
    for copy in w_in:
        copy.wait()
    c_sib.wait_recv()
    prep(0, 1 - c)
    ring_b[0].start()
    sum_a.block(0, get_a(0))
    c_1a.wait_recv()
    c_r1 = net.send(act.at[3, c, top], act.at[2, c, top], me.at_x(1))
    c_2a.wait_recv()
    c_r2 = net.send(act.at[1, c, low], act.at[2, c, low], me.at_x(-1))
    ring_b[0].mid()
    c_1b.wait_recv()
    c_s3 = net.send(act.at[3, c], act.at[3, c], me.sibling)
    c_2b.wait_recv()
    c_s1 = net.send(act.at[1, c], act.at[1, c], me.sibling)
    prep(3, c)
    prep(1, c)
    c_s3.wait_recv()
    prep(3, 1 - c)
    ring_b[3].start()
    sum_a.block(3, get_a(3))
    c_s1.wait_recv()
    prep(1, 1 - c)
    ring_b[1].start()
    sum_a.block(1, get_a(1))
    k_in, v_in = fetch(k_h.at[0], kv), fetch(v_h.at[0], vv)
    wo_in = fetch(wo_h, wo)
    sum_a.mid(0)
    sum_b.block(0, lambda j: ring_b[0].finish())
    c_r1.wait_recv()
    c_r2.wait_recv()
    c_s2 = net.send(act.at[2, c], act.at[2, c], me.sibling)
    prep(2, c)
    ring_b[3].mid()
    ring_b[1].mid()
    c_s2.wait_recv()
    prep(2, 1 - c)
    ring_b[2].start()
    sum_a.block(2, get_a(2))
    sum_a.mid(3)
    sum_a.mid(1)
    sq1 = [
        net.send(sqall.at[wrap(y + step)], sqr1.at[step - 1], me.at_y(step)) for step in range(1, 4)
    ]
    sum_b.block(3, lambda j: ring_b[3].finish())
    sum_b.block(1, lambda j: ring_b[1].finish())
    sum_b.mid(0)
    ring_b[2].mid()
    sum_a.mid(2)
    for copy in sq1:
        copy.wait_recv()
    sqs[...] = (sqall[y] + sqr1[0]) + (sqr1[1] + sqr1[2])
    sq2 = [net.send(sqs, sqr2.at[step - 1], me.at_z(step)) for step in range(1, 4)]
    sum_b.mid(3)
    sum_b.mid(1)
    sum_b.block(2, lambda j: ring_b[2].finish())
    ring_a2.start()
    for copy in sq2:
        copy.wait_recv()
    sqr1[0] = (sqs[...] + sqr2[0]) + (sqr2[1] + sqr2[2])
    own_sq = sqr1[0, pl.ds(z, 1), :]
    inverse = jnp.transpose(jnp.broadcast_to(lax.rsqrt(own_sq / D + 1e-05), (128, 128)))
    tab_in.wait()
    for copy in c_tab:
        copy.wait_recv()
    both = tab[...].reshape(128, 128)
    turned = pltpu.roll(both, 64, 1)
    first = lax.broadcasted_iota(jnp.int32, (128, 128), 1) < 64
    cosine = jnp.where(first, both, turned)
    sine = jnp.where(first, -turned, both)
    slots = lax.broadcasted_iota(jnp.int32, (8, CTX), 1)
    bias[...] = jnp.where(slots < len_ref[0], 0.0, -1e30)
    sum_b.mid(2)
    ring_a2.mid()

    def put(part, col, block):
        sendq[part, :, :, pl.ds(col, 128)] = block.astype(BF).reshape(8, 16, 128)

    def rotated(block):
        block = block * inverse
        return block * cosine + pltpu.roll(block, 64, 1) * sine

    def pass_on(part):
        recvq[part, gy] = sendq[part, gy]
        return [
            net.send(sendq.at[part, wrap(gy + step, 8)], recvq.at[part, gy], me.at_gy(step))
            for step in range(1, 8)
        ]

    fin = sum_b.finish(0)
    for head in range(4):
        put(1, head * 128, rotated(fin[:, head * 128 : (head + 1) * 128]))
    put(1, 512, fin[:, 512:640] * inverse)
    pass_b = pass_on(1)
    fin = ring_a2.finish()
    for head in range(5):
        put(0, head * 128, rotated(fin[:, head * 128 : (head + 1) * 128]))
    pass_a = pass_on(0)

    scale = HD ** (-0.5) * 1.4426950408889634
    contract = (((1,), (1,)), ((), ()))
    token = lax.rem(lax.broadcasted_iota(jnp.int32, (128, 16), 0), 16)
    causal = lax.broadcasted_iota(jnp.int32, (128, 16), 1) <= token
    spot = pl.ds(pl.multiple_of(lax.rem(gy, 4) * 16, 16), 16)
    home = g.at[lax.div(gy, 4), 0, 0, spot]
    k_in.wait()
    v_in.wait()

    def attend(group):
        left, right = recvq[0, group], recvq[1, group]
        query = jnp.concatenate(
            [left[:, h * 128 : (h + 1) * 128] for h in range(4)]
            + [right[:, h * 128 : (h + 1) * 128] for h in range(4)],
            axis=0,
        )
        lanes = pl.ds(pl.multiple_of(group * 128, 128), 128)
        new = lax.dot_general(query, left[:, 512:640], contract, preferred_element_type=F32)
        new = jnp.where(causal, new, -1e30)
        peak = jnp.full((128, CHUNK), -1e30, F32)
        for at in range(0, CTX, CHUNK):
            old = lax.dot_general(
                query, kv[pl.ds(at, CHUNK), lanes], contract, preferred_element_type=F32
            )
            old = (old.reshape(16, 8, CHUNK) + bias[:, pl.ds(at, CHUNK)]).reshape(128, CHUNK)
            score[:, pl.ds(at, CHUNK)] = old
            peak = jnp.maximum(peak, old)
        highest = jnp.maximum(
            jnp.max(peak, axis=1, keepdims=True), jnp.max(new, axis=1, keepdims=True)
        )
        new = jnp.exp2((new - highest) * scale)
        blend = jnp.dot(new.astype(BF), right[:, 512:640], preferred_element_type=F32)
        sums = jnp.zeros((128, CHUNK), F32)
        for at in range(0, CTX, CHUNK):
            old = jnp.exp2((score[:, pl.ds(at, CHUNK)] - highest) * scale)
            sums = sums + old
            blend = blend + jnp.dot(
                old.astype(BF), vv[pl.ds(at, CHUNK), lanes], preferred_element_type=F32
            )
        total = jnp.sum(sums, axis=1, keepdims=True) + jnp.sum(new, axis=1, keepdims=True)
        result = (blend / total).astype(BF)
        return jnp.concatenate([result[h * 16 : (h + 1) * 16] for h in range(8)], axis=1)

    home[...] = attend(gy)
    swap = []
    for step in range(1, 8):
        pass_a[step - 1].wait_recv()
        pass_b[step - 1].wait_recv()
        att[step] = attend(wrap(gy - step + 8, 8))
        swap.append(net.send(att.at[step], home, me.at_gy(-step)))

    a1 = RingCast(net, [g.at[0, k, 0] for k in range(4)], zp, zm)
    b1 = RingCast(net, [g.at[1, 0, k] for k in range(4)], yp, ym)
    a2 = [RingCast(net, [g.at[0, j, k] for k in range(4)], yp, ym) for j in range(4)]
    b2 = [RingCast(net, [g.at[1, k, j] for k in range(4)], zp, zm) for j in range(4)]
    mine = [lax.div(wrap(y + dy), 2) == c for dy in range(4)]
    pair = [net.make(sib_send.at[dy], sib_recv.at[dy], me.sibling, False) for dy in range(4)]

    def get_x(dy):
        def get(role):
            return sib_send[dy, role].astype(F32) + sib_recv[dy, role].astype(F32)
        return get

    ring_x = [
        RingSum(net, get_x(dy), me.at_x(1), me.at_x(-1), bufs_x, dy, 128, False) for dy in range(4)
    ]

    def multiply(dy):
        for half in range(2):
            rows = jnp.concatenate(
                [g[half, wrap(x + role - z + 4), dy] for role in range(4)], axis=0
            )
            term = jnp.dot(rows, wo[...], preferred_element_type=F32).astype(BF)
            for role in range(4):
                sib_send[dy, role, pl.ds(half * 64, 64), :] = term[role * 64 : (role + 1) * 64]

        @pl.when(jnp.logical_not(mine[dy]))
        def _():
            pair[dy].start()

    def sum_start(dy):
        @pl.when(mine[dy])
        def _():
            pair[dy].wait_recv()
            ring_x[dy].start()

    def sum_mid(dy):
        @pl.when(mine[dy])
        def _():
            ring_x[dy].mid()

    def sum_finish(dy):
        @pl.when(mine[dy])
        def _():
            rows = pl.ds(pl.multiple_of(lax.rem(wrap(y + dy), 2) * 128, 128), 128)
            out_ref[rows, :] = ring_x[dy].finish().astype(BF)
            for copy in ring_x[dy].copies:
                copy.wait_send()

        @pl.when(jnp.logical_not(mine[dy]))
        def _():
            pair[dy].wait_send()

    for copy in swap:
        copy.wait_recv()
    a1.start()
    b1.start()
    a2[0].start()
    b2[0].start()
    a1.relay()
    b1.relay()
    a1.near()
    b1.near()
    b2[0].relay()
    a2[1].start()
    a2[3].start()
    b2[1].start()
    b2[3].start()
    a1.far()
    a2[2].start()
    b1.far()
    b2[1].relay()
    b2[3].relay()
    a2[0].relay()
    b2[2].start()
    wo_in.wait()
    b2[0].near()
    b2[0].far()
    multiply(0)
    a2[1].relay()
    a2[3].relay()
    b2[2].relay()
    a2[2].relay()
    sum_start(0)
    for ring in a2:
        ring.near()
    b2[1].near()
    b2[1].far()
    multiply(1)
    sum_mid(0)
    b2[3].near()
    b2[3].far()
    sum_start(1)
    multiply(3)
    sum_start(3)
    sum_mid(1)
    for ring in a2:
        ring.far()
    b2[2].near()
    b2[2].far()
    multiply(2)
    sum_mid(3)
    sum_start(2)
    sum_finish(0)
    sum_finish(1)
    sum_finish(3)
    sum_mid(2)
    sum_finish(2)
    net.drain()
    assert net.count == COPIES, net.count
    assert len(local) == 9


def layer(act, gain, wq, wk, wv, wo, tab, lengths, key_cache, value_cache):
    hbm = pl.BlockSpec(memory_space=pl.ANY)
    vmem = pl.BlockSpec(memory_space=pltpu.VMEM)
    smem = pl.BlockSpec(memory_space=pltpu.SMEM)
    return pl.pallas_call(
        layer_kernel,
        out_shape=jax.ShapeDtypeStruct((256, 512), BF),
        in_specs=[hbm, vmem, hbm, hbm, hbm, hbm, hbm, smem, hbm, hbm],
        out_specs=vmem,
        scratch_shapes=[
            pltpu.VMEM((4, 2, 256, 512), BF),
            pltpu.VMEM((4, 2, 256, 512), BF),
            pltpu.VMEM((512, 1280), BF),
            pltpu.VMEM((8, 16, 128), F32),
            pltpu.VMEM((4, 8, 128), F32),
            pltpu.VMEM((3, 8, 128), F32),
            pltpu.VMEM((8, 128), F32),
            pltpu.VMEM((3, 8, 128), F32),
            pltpu.VMEM((2, 8, 16, COLS), BF),
            pltpu.VMEM((2, 8, 16, COLS), BF),
            pltpu.VMEM((CTX, 1024), BF),
            pltpu.VMEM((CTX, 1024), BF),
            pltpu.VMEM((8, CTX), F32),
            pltpu.VMEM((128, CTX), F32),
            pltpu.VMEM((8, 16, 1024), BF),
            pltpu.VMEM((2, 4, 4, 64, 1024), BF),
            pltpu.VMEM((1024, 512), BF),
            pltpu.VMEM((4, 4, 128, 512), BF),
            pltpu.VMEM((4, 4, 128, 512), BF),
            pltpu.VMEM((4, 1, 128, COLS), F32),
            *block_scratch(4, 128, COLS),
            *block_scratch(1, 128, COLS),
            *ring_scratch(4, 128, COLS),
            *ring_scratch(1, 128, COLS),
            *ring_scratch(4, 128, 512),
            pltpu.SemaphoreType.DMA((COPIES,)),
            pltpu.SemaphoreType.DMA((COPIES,)),
            pltpu.SemaphoreType.DMA((9,)),
        ],
        compiler_params=pltpu.CompilerParams(
            collective_id=0, has_side_effects=True, vmem_limit_bytes=60 * 1024 * 1024
        ),
        name="layer",
    )(act, gain, wq, wk, wv, wo, tab, lengths, key_cache, value_cache)


def places_table(position):
    frequency = jnp.exp(
        jnp.arange(64, dtype=F32) * (-2.0 * math.log(500000.0) / HD)
    )
    places = position + jnp.arange(DRAFT, dtype=jnp.int32)
    angles = places.astype(F32)[:, None] * frequency
    return jnp.concatenate([jnp.cos(angles), jnp.sin(angles)], axis=-1)


def shards(act, gain, wq, wk, wv, wo, key_cache, value_cache, lengths, positions):
    out = layer(
        act.reshape(256, 512), gain.reshape(1, 512), wq, wk, wv, wo,
        places_table(positions), lengths, key_cache, value_cache,
    )
    return out.reshape(16, DRAFT, 512)


def solution(mesh):
    return jax.shard_map(
        shards,
        mesh=mesh,
        in_specs=(
            P("gy", None, "gx"),
            P("gx"),
            P("gx", "gy"),
            P("gx", "gy"),
            P("gx", "gy"),
            P("gy", "gx"),
            P(("gx", "gy"), None, None),
            P(("gx", "gy"), None, None),
            P(("gx", "gy")),
            P(("gx", "gy")),
        ),
        out_specs=P("gy", None, "gx"),
        check_vma=False,
    )
```

time: 199 us -> 114 us (0.57); the launches traced: 196 us -> 114 us
  waiting for transfers between devices: 78.6 us -> 0 us
  Pallas kernels: 79.3 us -> 109 us
  between operations: 14.8 us -> 1.32 us
  blocking collectives: 10.8 us -> 0 us
  matrix products: 8.86 us -> 0 us
    all_gather x1 -> x0, waiting for transfers between devices: 48.2 us -> none  [shards(): gathered = lax.all_gather(regrouped, 'gx', axis=0, tiled=True)]
    reduce_scatter x1 -> x0, waiting for transfers between devices: 30.4 us -> none  [shards(): lax.psum_scatter(terms.astype(BF), 'gy', scatter_dimension=0, tiled=True)]
    pallas_call x2 -> x1, Pallas kernels: 79.3 us -> 109 us  [layer(): pl.pallas_call(layer_kernel, out_shape=jax.ShapeDtypeStruct((256, 512), B...]
    all_to_all x1 -> x0, blocking collectives: 10.8 us -> none  [shards(): lax.all_to_all(attended, 'gy', split_axis=0, concat_axis=0, tiled=True)]
    dot_general x1 -> x0, matrix products: 8.86 us -> none  [shards(): terms = jnp.einsum('btf,fd->btd', gathered, wo, preferred_element_type=F32)]
  transfers between devices with their start and end apart: 2 -> 0, of which waited for: 2 -> 0; matrix products, arithmetic and copies ran while one was open for 0% -> 0% of each run, Pallas kernels for 0% -> 0%
where the time goes in v3:
time: 114 us
  Pallas kernels  109 us (96%)
  local copies, waits for them, and re-layouts  2.93 us (3%)
  between operations  1.32 us (1%)
    pallas_call x1, Pallas kernels, layer(): pl.pallas_call(layer_kernel, out_shape=jax.ShapeDtypeStruct((256, 512), B...  109 us

profile of v3, /device:TPU:1, one launch (start us, length us, event | category | flops | bytes accessed | tf_op | source)
XLA Modules:
  0.0 113.7 jit_solution(16064075959031202181)
XLA Ops:
  1.3 1.3 %reshape.20.gain_ref = bf16[1,512]{1,0:T(2,128)(2,1)} reshape(bf16[512]{0:T(512)(128)(2,1)} %param.11) | data formatting | bytes 2048 | tf_op jit(solution)/shard_map/reshape | solution.py:660
  2.6 0.1 multiply_cosine_fusion
  2.7 0.7 pad_maximum_fusion.tab_h
  3.4 108.6 %layer.1 = bf16[256,512]{1,0:T(8,128)(2,1)} custom-call(bf16[256,512]{1,0:T(8,128)(2,1)} %bitcast.5, bf16[1,512]{1,0:T(2,128)(2,1)} %reshape.20.gain_ref, bf16[512,1024]{1,0:T(8,128)(2,1)} %wq_h.1, bf16[512,128]{1,0:T(8,128)(2,1)} %wk_h.1, bf16[512,128]{1,0:T(8,128)(2,1)} %wv_h.1, bf16[1024,512]{1,0:T(8,128)(2,1)} %wo_h.1, f32[16,128]{1,0:T(8,128)} %pad_maximum_fusion.tab_h, ...), custom_call_target="tpu_custom_call" | custom-call | tf_op jit(solution)/shard_map/layer/pallas_call | solution.py:607
  112.0 1.7 %copy.14 = bf16[16,16,512]{2,1,0:T(8,128)(2,1)} copy(bf16[16,16,512]{2,1,0:T(8,128)(2,1)} %bitcast.4) | data formatting | bytes 524288
  (2 shorter events, 0.0 us)

commit v4 on v3

v4 whole, which is shorter than its diff:
```python
import jax
import jax.numpy as jnp
import numpy as np
from jax import lax
from jax.experimental import pallas as pl
from jax.experimental.pallas import tpu as pltpu
from jax.sharding import PartitionSpec as P

D = 8192
HD = 128
KV = 8
CTX = 4096
DRAFT = 16
MESH = pl.DeviceIdType.MESH
F32 = jnp.float32
BF = jnp.bfloat16


def wrap(value, size=4):
    return lax.rem(value + size, size)


class Place:
    def __init__(self):
        gx, gy = lax.axis_index("gx"), lax.axis_index("gy")
        self.gx, self.gy = gx, gy
        self.z, self.y = lax.div(gx, 4), lax.rem(gx, 4)
        self.x, self.c = lax.div(gy, 2), lax.rem(gy, 2)
        self.sibling = (gx, gy + 1 - 2 * self.c)

    def at_x(self, step):
        return (self.gx, wrap(self.x + step) * 2 + self.c)

    def at_y(self, step):
        return (self.z * 4 + wrap(self.y + step), self.gy)

    def at_z(self, step):
        return (wrap(self.z + step) * 4 + self.y, self.gy)

    def at_gy(self, step):
        return (self.gx, wrap(self.gy + step, 8))


class Net:
    def __init__(self, send_sem, recv_sem):
        self.send_sem, self.recv_sem = send_sem, recv_sem
        self.count = 0
        self.sent = []

    def make(self, src, dst, device, drained=True):
        copy = pltpu.make_async_remote_copy(
            src_ref=src,
            dst_ref=dst,
            send_sem=self.send_sem.at[self.count],
            recv_sem=self.recv_sem.at[self.count],
            device_id=device,
            device_id_type=MESH,
        )
        self.count += 1
        if drained:
            self.sent.append(copy)
        return copy

    def send(self, src, dst, device):
        copy = self.make(src, dst, device)
        copy.start()
        return copy

    def drain(self):
        for copy in self.sent:
            copy.wait_send()


def greet(devices):
    barrier = pltpu.get_barrier_semaphore()
    for device in devices:
        pl.semaphore_signal(barrier, inc=1, device_id=device, device_id_type=MESH)
    pl.semaphore_wait(barrier, len(devices))


class RingSum:
    def __init__(self, net, get, plus, minus, bufs, lead, rows, drained=True):
        self.get = get
        self.rows, self.half = rows, rows // 2
        self.so, self.sp, self.sm, self.rom, self.rop, self.rdm, self.rdp, self.kp, self.km = [
            buf.at[lead] for buf in bufs
        ]
        lo, hi = pl.ds(0, self.half), pl.ds(self.half, self.half)
        self.lo, self.hi = lo, hi
        self.om = net.make(self.so.at[lo], self.rom, plus, drained)
        self.op = net.make(self.so.at[hi], self.rop, minus, drained)
        self.m1 = net.make(self.sp.at[hi], self.rdm.at[hi], plus, drained)
        self.p1 = net.make(self.sm.at[lo], self.rdp.at[lo], minus, drained)
        self.m2 = net.make(self.sp.at[lo], self.rdm.at[lo], plus, drained)
        self.p2 = net.make(self.sm.at[hi], self.rdp.at[hi], minus, drained)
        self.copies = [self.om, self.op, self.m1, self.p1, self.m2, self.p2]

    def start_far(self):
        self.so[...] = self.get(2).astype(BF)
        self.om.start()
        self.op.start()

    def start_near(self):
        h = self.half
        part = self.get(1)
        self.kp[...] = part[:h]
        self.sp[self.hi] = part[h:].astype(BF)
        self.m1.start()
        part = self.get(3)
        self.km[...] = part[h:]
        self.sm[self.lo] = part[:h].astype(BF)
        self.p1.start()

    def mid(self):
        self.om.wait_recv()
        self.sp[self.lo] = (self.kp[...] + self.rom[...].astype(F32)).astype(BF)
        self.m2.start()
        self.op.wait_recv()
        self.sm[self.hi] = (self.km[...] + self.rop[...].astype(F32)).astype(BF)
        self.p2.start()

    def finish(self):
        own = self.get(0)
        for copy in (self.m1, self.p1, self.m2, self.p2):
            copy.wait_recv()
        return own + self.rdm[...].astype(F32) + self.rdp[...].astype(F32)


class DirectSum:
    def __init__(self, net, sources, devices, landing, drained=True):
        self.landing = landing
        self.copies = [
            net.make(src, landing.at[i], device, drained)
            for i, (src, device) in enumerate(zip(sources, devices))
        ]

    def finish(self, own):
        for copy in self.copies:
            copy.wait_recv()
        a, b, c = (self.landing[i].astype(F32) for i in range(3))
        return (own + a) + (b + c)


def ring_scratch(count, rows, cols):
    h = rows // 2
    return [
        pltpu.VMEM((count, rows, cols), BF),
        pltpu.VMEM((count, rows, cols), BF),
        pltpu.VMEM((count, rows, cols), BF),
        pltpu.VMEM((count, h, cols), BF),
        pltpu.VMEM((count, h, cols), BF),
        pltpu.VMEM((count, rows, cols), BF),
        pltpu.VMEM((count, rows, cols), BF),
        pltpu.VMEM((count, h, cols), F32),
        pltpu.VMEM((count, h, cols), F32),
    ]


class BlockSum:
    def __init__(self, net, role, slot, plus, minus, bufs, rows):
        self.role, self.slot = role, slot
        self.out, self.rom, self.rop, self.rdm, self.rdp = bufs
        h = rows // 2
        lo, hi = pl.ds(0, h), pl.ds(h, h)
        self.lo, self.hi = lo, hi
        far, near, last = slot(2), slot(1), slot(3)
        self.om = net.make(self.out.at[far, :, lo], self.rom, plus)
        self.op = net.make(self.out.at[far, :, hi], self.rop, minus)
        self.m1 = net.make(self.out.at[near, :, hi], self.rdm.at[:, hi], plus)
        self.p1 = net.make(self.out.at[last, :, lo], self.rdp.at[:, lo], minus)
        self.m2 = net.make(self.out.at[near, :, lo], self.rdm.at[:, lo], plus)
        self.p2 = net.make(self.out.at[last, :, hi], self.rdp.at[:, hi], minus)

    def block(self, k):
        role = self.role(k)

        @pl.when(role == 2)
        def _():
            self.om.start()
            self.op.start()

        @pl.when(role == 1)
        def _():
            self.m1.start()

        @pl.when(role == 3)
        def _():
            self.p1.start()

    def mid(self, k):
        role = self.role(k)

        @pl.when(role == 1)
        def _():
            self.om.wait_recv()
            total = self.out[k, :, self.lo].astype(F32) + self.rom[...].astype(F32)
            self.out[k, :, self.lo] = total.astype(BF)
            self.m2.start()

        @pl.when(role == 3)
        def _():
            self.op.wait_recv()
            total = self.out[k, :, self.hi].astype(F32) + self.rop[...].astype(F32)
            self.out[k, :, self.hi] = total.astype(BF)
            self.p2.start()

    def arrived(self):
        for copy in (self.m1, self.p1, self.m2, self.p2):
            copy.wait_recv()

    def finish(self, j):
        own = self.out[self.slot(0), j].astype(F32)
        return own + self.rdm[j].astype(F32) + self.rdp[j].astype(F32)


def block_scratch(parts, rows, cols):
    return [
        pltpu.VMEM((4, parts, rows, cols), BF),
        pltpu.VMEM((parts, rows // 2, cols), BF),
        pltpu.VMEM((parts, rows // 2, cols), BF),
        pltpu.VMEM((parts, rows, cols), BF),
        pltpu.VMEM((parts, rows, cols), BF),
    ]


class RingCast:
    def __init__(self, net, slots, plus, minus):
        lo, hi = pl.ds(0, 32), pl.ds(32, 32)
        own, next_, far, last = slots
        self.to_plus = net.make(own, last, plus)
        self.to_minus = net.make(own, next_, minus)
        self.on_plus = net.make(last.at[lo], far.at[lo], plus)
        self.on_minus = net.make(next_.at[hi], far.at[hi], minus)

    def start(self):
        self.to_plus.start()
        self.to_minus.start()

    def relay(self):
        self.to_plus.wait_recv()
        self.on_plus.start()
        self.to_minus.wait_recv()
        self.on_minus.start()

    def far(self):
        self.on_plus.wait_recv()
        self.on_minus.wait_recv()


COLS = 640
COPIES = 198
CHUNK = 1024


def layer_kernel(
    act_h, gain_ref, wq_h, wk_h, wv_h, wo_h, freq_ref, pos_ref, len_ref, k_h, v_h, out_ref,
    act, scaled, w, prod, tab, sqall, sqr1, sqs, sqr2, sendq, recvq, kv, vv, bias, score, att,
    g, wo, sib_send, sib_recv, keep_b, *rest,
):
    bufs_a = [rest[:5], rest[5:10]]
    bufs_b = [rest[10:19], rest[19:28]]
    out_b, in_b, out_a2, in_a2, out_x, in_x, send_sem, recv_sem, local_sem = rest[28:]
    me = Place()
    x, c, y, z, gy = me.x, me.c, me.y, me.z, me.gy
    net = Net(send_sem, recv_sem)
    ym, yp, zm, zp = me.at_y(-1), me.at_y(1), me.at_z(-1), me.at_z(1)

    local = []

    def fetch(src, dst):
        copy = pltpu.make_async_copy(src, dst, local_sem.at[len(local)])
        copy.start()
        local.append(copy)
        return copy

    own_in = fetch(act_h, act.at[0, c])
    w_in = [
        fetch(wq_h.at[:, pl.ds(0, 512)], w.at[:, pl.ds(0, 512)]),
        fetch(wk_h, w.at[:, pl.ds(512, 128)]),
        fetch(wq_h.at[:, pl.ds(512, 512)], w.at[:, pl.ds(640, 512)]),
        fetch(wv_h, w.at[:, pl.ds(1152, 128)]),
    ]
    token = lax.broadcasted_iota(jnp.int32, (DRAFT, HD), 0)
    angles = (pos_ref[0] + token).astype(F32) * freq_ref[...]
    half = lax.broadcasted_iota(jnp.int32, (DRAFT, HD), 1) < HD // 2
    tab[gy] = jnp.where(half, jnp.cos(angles), jnp.sin(angles))

    greet(
        [me.at_gy(step) for step in range(1, 8)]
        + [me.at_y(step) for step in range(1, 4)]
        + [me.at_z(step) for step in range(1, 4)]
    )

    span = (pl.ds(0, 64), pl.ds(64, 64))
    c_sib, c_pj, c_mj, c_rp, c_rm, c_s = [], [], [], [], [], [{}, {}]

    def to_neighbours(h):
        c_pj.append([None, None])
        c_mj.append([None, None])
        for j in range(2):
            src = act_h.at[j, span[h]]
            c_pj[h][j] = net.send(src, act.at[3, c, j, span[h]], me.at_x(1))
            src = act_h.at[1 - j, span[h]]
            c_mj[h][1 - j] = net.send(src, act.at[1, c, 1 - j, span[h]], me.at_x(-1))

    def to_sibling(slot, h):
        part = act.at[slot, c, :, span[h]]
        c_s[h][slot] = net.send(part, part, me.sibling)

    def relay(h):
        c_pj[h][0].wait_recv()
        c_rp.append(net.send(act.at[3, c, 0, span[h]], act.at[2, c, 0, span[h]], me.at_x(1)))
        c_mj[h][1].wait_recv()
        c_rm.append(net.send(act.at[1, c, 1, span[h]], act.at[2, c, 1, span[h]], me.at_x(-1)))

    def near(h):
        c_pj[h][1].wait_recv()
        to_sibling(3, h)
        c_mj[h][0].wait_recv()
        to_sibling(1, h)

    def far(h):
        c_rp[h].wait_recv()
        c_rm[h].wait_recv()
        to_sibling(2, h)

    for h in range(2):
        c_sib.append(net.send(act_h.at[:, span[h]], act.at[0, c, :, span[h]], me.sibling))
    to_neighbours(0)
    c_tab = [net.send(tab.at[gy], tab.at[gy], me.at_gy(step)) for step in range(1, 8)]

    gain = gain_ref[...].astype(F32).reshape(1, 512)

    def prep(slot, core, h):
        for j in range(2):
            wide = act[slot, core, j, span[h], :].astype(F32)
            scaled[slot, h, 2 * core + j] = (wide * gain).astype(BF)
            square = wide * wide
            fold = (square[:, 0:128] + square[:, 128:256]) + (square[:, 256:384] + square[:, 384:512])
            row = jnp.sum(jnp.transpose(fold), axis=0, keepdims=True)
            sqall[h, 2 * core + j, pl.ds(wrap(x + slot), 1), pl.ds(0, 64)] = row

    def get_b(slot, h):
        def get(role):
            return prod[h, slot, wrap(y + role)]
        return get

    def role_z(slot):
        return wrap(x + slot - z + 4)

    def slot_z(role):
        return wrap(z + role - x + 4)

    ring_b = [
        [RingSum(net, get_b(k, h), yp, ym, bufs_b[h], k, 64) for k in range(4)] for h in range(2)
    ]
    sum_a = [BlockSum(net, role_z, slot_z, zp, zm, bufs_a[h], 64) for h in range(2)]
    sum_b = [
        DirectSum(
            net, [out_b.at[h, slot_z(r)] for r in (1, 2, 3)], [me.at_z(r) for r in (1, 2, 3)],
            in_b.at[h],
        )
        for h in range(2)
    ]
    sum_a2 = [
        DirectSum(
            net, [out_a2.at[h, r - 1] for r in (1, 2, 3)], [me.at_y(r) for r in (1, 2, 3)],
            in_a2.at[h],
        )
        for h in range(2)
    ]

    def multiply_in(k, h):
        rows = scaled[k, h].reshape(256, 512)
        term = jnp.dot(rows, w[:, COLS:], preferred_element_type=F32)
        for j in range(4):
            prod[h, k, j] = term[j * 64 : (j + 1) * 64]
        ring_b[h][k].start_far()
        term = jnp.dot(rows, w[:, :COLS], preferred_element_type=F32).astype(BF)
        for j in range(4):
            sum_a[h].out[k, wrap(j - y)] = term[j * 64 : (j + 1) * 64]
        sum_a[h].block(k)
        ring_b[h][k].start_near()

    def block_b(slot, h):
        value = ring_b[h][slot].finish()
        keep_b[h, slot] = value
        out_b[h, slot] = value.astype(BF)
        for r in (1, 2, 3):

            @pl.when(role_z(slot) == r)
            def _():
                sum_b[h].copies[r - 1].start()

    def part_a2(h):
        sum_a[h].arrived()
        for r in (2, 1, 3):
            out_a2[h, r - 1] = sum_a[h].finish(r).astype(BF)
            sum_a2[h].copies[r - 1].start()

    own_in.wait()
    prep(0, c, 0)
    for copy in w_in:
        copy.wait()
    c_sib[0].wait_recv()
    prep(0, 1 - c, 0)
    multiply_in(0, 0)
    relay(0)
    to_neighbours(1)
    prep(0, c, 1)
    c_sib[1].wait_recv()
    prep(0, 1 - c, 1)
    multiply_in(0, 1)
    near(0)
    ring_b[0][0].mid()
    prep(3, c, 0)
    prep(1, c, 0)
    c_s[0][3].wait_recv()
    prep(3, 1 - c, 0)
    multiply_in(3, 0)
    c_s[0][1].wait_recv()
    prep(1, 1 - c, 0)
    multiply_in(1, 0)
    far(0)
    relay(1)
    prep(2, c, 0)
    c_s[0][2].wait_recv()
    prep(2, 1 - c, 0)
    multiply_in(2, 0)
    near(1)
    sum_a[0].mid(0)
    ring_b[1][0].mid()
    ring_b[0][3].mid()
    ring_b[0][1].mid()
    block_b(0, 0)
    prep(3, c, 1)
    prep(1, c, 1)
    c_s[1][3].wait_recv()
    prep(3, 1 - c, 1)
    multiply_in(3, 1)
    c_s[1][1].wait_recv()
    prep(1, 1 - c, 1)
    multiply_in(1, 1)
    far(1)
    sum_a[0].mid(3)
    sum_a[0].mid(1)
    ring_b[0][2].mid()
    prep(2, c, 1)
    c_s[1][2].wait_recv()
    prep(2, 1 - c, 1)
    multiply_in(2, 1)
    k_in, v_in = fetch(k_h.at[0], kv), fetch(v_h.at[0], vv)
    wo_in = fetch(wo_h, wo)
    sq1 = [
        net.send(sqall.at[:, wrap(y + step)], sqr1.at[step - 1], me.at_y(step))
        for step in range(1, 4)
    ]
    block_b(3, 0)
    block_b(1, 0)
    sum_a[0].mid(2)
    sum_a[1].mid(0)
    block_b(0, 1)
    ring_b[1][3].mid()
    ring_b[1][1].mid()
    block_b(2, 0)
    sum_a[1].mid(3)
    sum_a[1].mid(1)
    ring_b[1][2].mid()
    for copy in sq1:
        copy.wait_recv()
    sqs[...] = (sqall[:, y] + sqr1[0]) + (sqr1[1] + sqr1[2])
    sq2 = [net.send(sqs, sqr2.at[step - 1], me.at_z(step)) for step in range(1, 4)]
    part_a2(0)
    sum_a[1].mid(2)
    block_b(3, 1)
    block_b(1, 1)
    block_b(2, 1)
    part_a2(1)
    for copy in sq2:
        copy.wait_recv()
    sqr1[0] = (sqs[...] + sqr2[0]) + (sqr2[1] + sqr2[2])
    halves = [
        jnp.transpose(
            jnp.broadcast_to(lax.rsqrt(sqr1[0, h, pl.ds(z, 1), :] / D + 1e-05), (128, 128))
        )[:64]
        for h in range(2)
    ]
    for copy in c_tab:
        copy.wait_recv()
    inverse = jnp.concatenate(halves, axis=0)
    both = tab[...].reshape(128, 128)
    turned = pltpu.roll(both, 64, 1)
    first = lax.broadcasted_iota(jnp.int32, (128, 128), 1) < 64
    cosine = jnp.where(first, both, turned)
    sine = jnp.where(first, -turned, both)
    slots = lax.broadcasted_iota(jnp.int32, (8, CTX), 1)
    bias[...] = jnp.where(slots < len_ref[0], 0.0, -1e30)

    def put(part, col, block):
        sendq[part, :, :, pl.ds(col, 128)] = block.astype(BF).reshape(8, 16, 128)

    def rotated(block):
        block = block * inverse
        return block * cosine + pltpu.roll(block, 64, 1) * sine

    partners = []
    for xx, cc in (
        (x, 1 - c),
        (x + 1 - 2 * lax.rem(x, 2), c),
        (3 - x, c),
        (wrap(x + 2), c),
        (wrap(x + 2), 1 - c),
        (x + 1 - 2 * lax.rem(x, 2), 1 - c),
        (3 - x, 1 - c),
    ):
        partners.append(xx * 2 + cc)

    def pass_on(part):
        recvq[part, gy] = sendq[part, gy]
        return [
            net.send(sendq.at[part, other], recvq.at[part, gy], (me.gx, other))
            for other in partners
        ]

    fin = jnp.concatenate([sum_b[h].finish(keep_b[h, slot_z(0)]) for h in range(2)], axis=0)
    for head in range(4):
        put(1, head * 128, rotated(fin[:, head * 128 : (head + 1) * 128]))
    put(1, 512, fin[:, 512:640] * inverse)
    pass_b = pass_on(1)
    fin = jnp.concatenate([sum_a2[h].finish(sum_a[h].finish(0)) for h in range(2)], axis=0)
    for head in range(5):
        put(0, head * 128, rotated(fin[:, head * 128 : (head + 1) * 128]))
    pass_a = pass_on(0)

    scale = HD ** (-0.5) * 1.4426950408889634
    contract = (((1,), (1,)), ((), ()))
    draft = lax.rem(lax.broadcasted_iota(jnp.int32, (128, 16), 0), 16)
    causal = lax.broadcasted_iota(jnp.int32, (128, 16), 1) <= draft
    spot = pl.ds(pl.multiple_of(lax.rem(gy, 4) * 16, 16), 16)
    home = g.at[lax.div(gy, 4), 0, 0, spot]
    k_in.wait()
    v_in.wait()

    def attend(group):
        left, right = recvq[0, group], recvq[1, group]
        query = jnp.concatenate(
            [left[:, h * 128 : (h + 1) * 128] for h in range(4)]
            + [right[:, h * 128 : (h + 1) * 128] for h in range(4)],
            axis=0,
        )
        lanes = pl.ds(pl.multiple_of(group * 128, 128), 128)
        new = lax.dot_general(query, left[:, 512:640], contract, preferred_element_type=F32)
        new = jnp.where(causal, new, -1e30)
        peak = jnp.full((128, CHUNK), -1e30, F32)
        for at in range(0, CTX, CHUNK):
            old = lax.dot_general(
                query, kv[pl.ds(at, CHUNK), lanes], contract, preferred_element_type=F32
            )
            old = (old.reshape(16, 8, CHUNK) + bias[:, pl.ds(at, CHUNK)]).reshape(128, CHUNK)
            score[:, pl.ds(at, CHUNK)] = old
            peak = jnp.maximum(peak, old)
        highest = jnp.maximum(
            jnp.max(peak, axis=1, keepdims=True), jnp.max(new, axis=1, keepdims=True)
        )
        new = jnp.exp2((new - highest) * scale)
        blend = jnp.dot(new.astype(BF), right[:, 512:640], preferred_element_type=F32)
        sums = jnp.zeros((128, CHUNK), F32)
        for at in range(0, CTX, CHUNK):
            old = jnp.exp2((score[:, pl.ds(at, CHUNK)] - highest) * scale)
            sums = sums + old
            blend = blend + jnp.dot(
                old.astype(BF), vv[pl.ds(at, CHUNK), lanes], preferred_element_type=F32
            )
        total = jnp.sum(sums, axis=1, keepdims=True) + jnp.sum(new, axis=1, keepdims=True)
        result = (blend / total).astype(BF)
        return jnp.concatenate([result[h * 16 : (h + 1) * 16] for h in range(8)], axis=1)

    home[...] = attend(gy)
    swap = []
    for step, other in enumerate(partners):
        pass_a[step].wait_recv()
        pass_b[step].wait_recv()
        att[step] = attend(other)
        swap.append(net.send(att.at[step], home, (me.gx, other)))

    a1 = RingCast(net, [g.at[0, k, 0] for k in range(4)], zp, zm)
    b1 = RingCast(net, [g.at[1, 0, k] for k in range(4)], yp, ym)
    a2 = [RingCast(net, [g.at[0, j, k] for k in range(4)], yp, ym) for j in range(4)]
    b2 = [RingCast(net, [g.at[1, k, j] for k in range(4)], zp, zm) for j in range(4)]
    mine = [lax.div(wrap(y + dy), 2) == c for dy in range(4)]
    pair = [
        [
            net.make(sib_send.at[dy, :, part], sib_recv.at[dy, :, part], me.sibling, False)
            for part in span
        ]
        for dy in range(4)
    ]
    sum_x = [
        [
            [
                net.make(out_x.at[dy, r - 1, part], in_x.at[dy, r - 1, part], me.at_x(r), False)
                for r in (1, 2, 3)
            ]
            for part in span
        ]
        for dy in range(4)
    ]

    def both_cores(dy, role, part):
        return sib_send[dy, role, part].astype(F32) + sib_recv[dy, role, part].astype(F32)

    def multiply(half, dy):
        rows = jnp.concatenate(
            [g[half, wrap(x + role - z + 4), dy] for role in range(4)], axis=0
        )
        term = jnp.dot(rows, wo[...], preferred_element_type=F32).astype(BF)
        for role in range(4):
            sib_send[dy, role, span[half], :] = term[role * 64 : (role + 1) * 64]

        @pl.when(jnp.logical_not(mine[dy]))
        def _():
            pair[dy][half].start()

    def sum_start(half, dy):
        @pl.when(mine[dy])
        def _():
            pair[dy][half].wait_recv()
            for r in (2, 1, 3):
                out_x[dy, r - 1, span[half]] = both_cores(dy, r, span[half]).astype(BF)
                sum_x[dy][half][r - 1].start()

    def sum_finish(dy):
        @pl.when(mine[dy])
        def _():
            base = lax.rem(wrap(y + dy), 2) * 128
            for half in range(2):
                for copy in sum_x[dy][half]:
                    copy.wait_recv()
                total = both_cores(dy, 0, span[half])
                for r in range(3):
                    total = total + in_x[dy, r, span[half]].astype(F32)
                rows = pl.ds(pl.multiple_of(base + half * 64, 64), 64)
                out_ref[rows, :] = total.astype(BF)
                for copy in sum_x[dy][half]:
                    copy.wait_send()

        @pl.when(jnp.logical_not(mine[dy]))
        def _():
            for copy in pair[dy]:
                copy.wait_send()

    for copy in swap:
        copy.wait_recv()
    a1.start()
    b1.start()
    a2[0].start()
    b2[0].start()
    a1.relay()
    b1.relay()
    for ring in (a2[1], b2[1], a2[3], b2[3]):
        ring.start()
    a2[0].relay()
    b2[0].relay()
    a1.far()
    b1.far()
    a2[2].start()
    b2[2].start()
    wo_in.wait()
    multiply(0, 0)
    for ring in (a2[1], b2[1], a2[3], b2[3]):
        ring.relay()
    b2[0].far()
    multiply(1, 0)
    sum_start(0, 0)
    a2[2].relay()
    multiply(0, 1)
    multiply(0, 3)
    sum_start(1, 0)
    b2[2].relay()
    b2[1].far()
    multiply(1, 1)
    sum_start(0, 1)
    sum_start(0, 3)
    b2[3].far()
    multiply(1, 3)
    sum_start(1, 1)
    for ring in a2:
        ring.far()
    multiply(0, 2)
    sum_start(1, 3)
    b2[2].far()
    multiply(1, 2)
    sum_start(0, 2)
    sum_start(1, 2)
    sum_finish(0)
    sum_finish(1)
    sum_finish(3)
    sum_finish(2)
    net.drain()
    assert net.count == COPIES, net.count
    assert len(local) == 8


def layer(act, gain, wq, wk, wv, wo, freq, positions, lengths, key_cache, value_cache):
    hbm = pl.BlockSpec(memory_space=pl.ANY)
    vmem = pl.BlockSpec(memory_space=pltpu.VMEM)
    smem = pl.BlockSpec(memory_space=pltpu.SMEM)
    return pl.pallas_call(
        layer_kernel,
        out_shape=jax.ShapeDtypeStruct((256, 512), BF),
        in_specs=[hbm, vmem, hbm, hbm, hbm, hbm, vmem, smem, smem, hbm, hbm],
        out_specs=vmem,
        scratch_shapes=[
            pltpu.VMEM((4, 2, 2, 128, 512), BF),
            pltpu.VMEM((4, 2, 4, 64, 512), BF),
            pltpu.VMEM((512, 1280), BF),
            pltpu.VMEM((2, 4, 4, 64, COLS), F32),
            pltpu.VMEM((8, 16, 128), F32),
            pltpu.VMEM((2, 4, 8, 128), F32),
            pltpu.VMEM((3, 2, 8, 128), F32),
            pltpu.VMEM((2, 8, 128), F32),
            pltpu.VMEM((3, 2, 8, 128), F32),
            pltpu.VMEM((2, 8, 16, COLS), BF),
            pltpu.VMEM((2, 8, 16, COLS), BF),
            pltpu.VMEM((CTX, 1024), BF),
            pltpu.VMEM((CTX, 1024), BF),
            pltpu.VMEM((8, CTX), F32),
            pltpu.VMEM((128, CTX), F32),
            pltpu.VMEM((7, 16, 1024), BF),
            pltpu.VMEM((2, 4, 4, 64, 1024), BF),
            pltpu.VMEM((1024, 512), BF),
            pltpu.VMEM((4, 4, 128, 512), BF),
            pltpu.VMEM((4, 4, 128, 512), BF),
            pltpu.VMEM((2, 4, 64, COLS), F32),
            *block_scratch(4, 64, COLS),
            *block_scratch(4, 64, COLS),
            *ring_scratch(4, 64, COLS),
            *ring_scratch(4, 64, COLS),
            pltpu.VMEM((2, 4, 64, COLS), BF),
            pltpu.VMEM((2, 3, 64, COLS), BF),
            pltpu.VMEM((2, 3, 64, COLS), BF),
            pltpu.VMEM((2, 3, 64, COLS), BF),
            pltpu.VMEM((4, 3, 128, 512), BF),
            pltpu.VMEM((4, 3, 128, 512), BF),
            pltpu.SemaphoreType.DMA((COPIES,)),
            pltpu.SemaphoreType.DMA((COPIES,)),
            pltpu.SemaphoreType.DMA((8,)),
        ],
        compiler_params=pltpu.CompilerParams(
            collective_id=0, has_side_effects=True, vmem_limit_bytes=60 * 1024 * 1024
        ),
        name="layer",
    )(act, gain, wq, wk, wv, wo, freq, positions, lengths, key_cache, value_cache)


def frequencies():
    power = np.arange(64, dtype=np.float64) * (-2.0 / HD)
    row = np.tile(np.power(500000.0, power), 2)
    return jnp.asarray(np.broadcast_to(row, (DRAFT, HD)).astype(np.float32))


def shards(act, gain, wq, wk, wv, wo, key_cache, value_cache, lengths, positions):
    out = layer(
        act.reshape(2, 128, 512), gain, wq, wk, wv, wo,
        frequencies(), positions, lengths, key_cache, value_cache,
    )
    return out.reshape(16, DRAFT, 512)


def solution(mesh):
    return jax.shard_map(
        shards,
        mesh=mesh,
        in_specs=(
            P("gy", None, "gx"),
            P("gx"),
            P("gx", "gy"),
            P("gx", "gy"),
            P("gx", "gy"),
            P("gy", "gx"),
            P(("gx", "gy"), None, None),
            P(("gx", "gy"), None, None),
            P(("gx", "gy")),
            P(("gx", "gy")),
        ),
        out_specs=P("gy", None, "gx"),
        check_vma=False,
    )
```

time: 114 us -> 105 us (0.921)
  Pallas kernels: 109 us -> 102 us
  local copies, waits for them, and re-layouts: 2.93 us -> 1.67 us
    pallas_call x1, Pallas kernels: 109 us -> 102 us  [layer(): pl.pallas_call(layer_kernel, out_shape=jax.ShapeDtypeStruct((256, 512), B...]
    reshape x1 -> x0, local copies, waits for them, and re-layouts: 1.26 us -> none  [shards(): gain.reshape(1, 512)]
where the time goes in v4:
time: 105 us
  Pallas kernels  102 us (97%)
  local copies, waits for them, and re-layouts  1.67 us (2%)
  between operations  1.31 us (1%)
    pallas_call x1, Pallas kernels, layer(): pl.pallas_call(layer_kernel, out_shape=jax.ShapeDtypeStruct((256, 512), B...  102 us

profile of v4, /device:TPU:1, one launch (start us, length us, event | category | flops | bytes accessed | tf_op | source)
XLA Modules:
  0.0 105.0 jit_solution(17307877550919154973)
XLA Ops:
  1.3 102.1 %layer.1 = bf16[256,512]{1,0:T(8,128)(2,1)} custom-call(bf16[2,128,512]{2,1,0:T(8,128)(2,1)} %bitcast.3, bf16[512]{0:T(512)(128)(2,1)} %gain_ref.1, bf16[512,1024]{1,0:T(8,128)(2,1)} %wq_h.1, bf16[512,128]{1,0:T(8,128)(2,1)} %wk_h.1, bf16[512,128]{1,0:T(8,128)(2,1)} %wv_h.1, bf16[1024,512]{1,0:T(8,128)(2,1)} %wo_h.1, f32[16,128]{1,0:T(8,128)} %constant.2.clone.freq_ref, ...), custom_call_target="tpu_custom_call" | custom-call | tf_op jit(solution)/shard_map/layer/pallas_call | solution.py:708
  103.4 1.7 %copy.15 = bf16[16,16,512]{2,1,0:T(8,128)(2,1)} copy(bf16[16,16,512]{2,1,0:T(8,128)(2,1)} %bitcast.2) | data formatting | bytes 524288

commit v5 on v4

--- a/solution.py
+++ b/solution.py
@@ -157,59 +157,67 @@
 
 
 class BlockSum:
-    def __init__(self, net, role, slot, plus, minus, bufs, rows):
-        self.role, self.slot = role, slot
+    def __init__(self, net, role, slot, plus, minus, bufs, parts, rows):
+        self.role, self.slot, self.parts = role, slot, parts
         self.out, self.rom, self.rop, self.rdm, self.rdp = bufs
         h = rows // 2
         lo, hi = pl.ds(0, h), pl.ds(h, h)
         self.lo, self.hi = lo, hi
         far, near, last = slot(2), slot(1), slot(3)
-        self.om = net.make(self.out.at[far, :, lo], self.rom, plus)
-        self.op = net.make(self.out.at[far, :, hi], self.rop, minus)
-        self.m1 = net.make(self.out.at[near, :, hi], self.rdm.at[:, hi], plus)
-        self.p1 = net.make(self.out.at[last, :, lo], self.rdp.at[:, lo], minus)
-        self.m2 = net.make(self.out.at[near, :, lo], self.rdm.at[:, lo], plus)
-        self.p2 = net.make(self.out.at[last, :, hi], self.rdp.at[:, hi], minus)
+        span = range(parts)
+        self.om = [net.make(self.out.at[far, j, lo], self.rom.at[j], plus) for j in span]
+        self.op = [net.make(self.out.at[far, j, hi], self.rop.at[j], minus) for j in span]
+        self.m1 = [net.make(self.out.at[near, j, hi], self.rdm.at[j, hi], plus) for j in span]
+        self.p1 = [net.make(self.out.at[last, j, lo], self.rdp.at[j, lo], minus) for j in span]
+        self.m2 = [net.make(self.out.at[near, j, lo], self.rdm.at[j, lo], plus) for j in span]
+        self.p2 = [net.make(self.out.at[last, j, hi], self.rdp.at[j, hi], minus) for j in span]
 
     def block(self, k):
         role = self.role(k)
 
         @pl.when(role == 2)
         def _():
-            self.om.start()
-            self.op.start()
+            for j in (2, 1, 3, 0):
+                self.om[j].start()
+                self.op[j].start()
 
         @pl.when(role == 1)
         def _():
-            self.m1.start()
+            for j in (2, 1, 3, 0):
+                self.m1[j].start()
 
         @pl.when(role == 3)
         def _():
-            self.p1.start()
+            for j in (2, 1, 3, 0):
+                self.p1[j].start()
+
+    def value(self, k, j, rows):
+        return self.out[k, j, rows].astype(F32)
 
     def mid(self, k):
         role = self.role(k)
+        order = (2, 1, 3, 0)
 
         @pl.when(role == 1)
         def _():
-            self.om.wait_recv()
-            total = self.out[k, :, self.lo].astype(F32) + self.rom[...].astype(F32)
-            self.out[k, :, self.lo] = total.astype(BF)
-            self.m2.start()
+            for j in order:
+                self.om[j].wait_recv()
+                total = self.value(k, j, self.lo) + self.rom[j].astype(F32)
+                self.out[k, j, self.lo] = total.astype(BF)
+                self.m2[j].start()
 
         @pl.when(role == 3)
         def _():
-            self.op.wait_recv()
-            total = self.out[k, :, self.hi].astype(F32) + self.rop[...].astype(F32)
-            self.out[k, :, self.hi] = total.astype(BF)
-            self.p2.start()
-
-    def arrived(self):
-        for copy in (self.m1, self.p1, self.m2, self.p2):
+            for j in order:
+                self.op[j].wait_recv()
+                total = self.value(k, j, self.hi) + self.rop[j].astype(F32)
+                self.out[k, j, self.hi] = total.astype(BF)
+                self.p2[j].start()
+
+    def finish(self, j):
+        own = self.value(self.slot(0), j, slice(None))
+        for copy in (self.m1[j], self.p1[j], self.m2[j], self.p2[j]):
             copy.wait_recv()
-
-    def finish(self, j):
-        own = self.out[self.slot(0), j].astype(F32)
         return own + self.rdm[j].astype(F32) + self.rdp[j].astype(F32)
 
 
@@ -225,7 +233,7 @@
 
 class RingCast:
     def __init__(self, net, slots, plus, minus):
-        lo, hi = pl.ds(0, 32), pl.ds(32, 32)
+        lo, hi = pl.ds(0, 16), pl.ds(16, 16)
         own, next_, far, last = slots
         self.to_plus = net.make(own, last, plus)
         self.to_minus = net.make(own, next_, minus)
@@ -248,7 +256,7 @@
 
 
 COLS = 640
-COPIES = 198
+COPIES = 274
 CHUNK = 1024
 
 
@@ -354,7 +362,7 @@
     ring_b = [
         [RingSum(net, get_b(k, h), yp, ym, bufs_b[h], k, 64) for k in range(4)] for h in range(2)
     ]
-    sum_a = [BlockSum(net, role_z, slot_z, zp, zm, bufs_a[h], 64) for h in range(2)]
+    sum_a = [BlockSum(net, role_z, slot_z, zp, zm, bufs_a[h], 4, 64) for h in range(2)]
     sum_b = [
         DirectSum(
             net, [out_b.at[h, slot_z(r)] for r in (1, 2, 3)], [me.at_z(r) for r in (1, 2, 3)],
@@ -393,7 +401,6 @@
                 sum_b[h].copies[r - 1].start()
 
     def part_a2(h):
-        sum_a[h].arrived()
         for r in (2, 1, 3):
             out_a2[h, r - 1] = sum_a[h].finish(r).astype(BF)
             sum_a2[h].copies[r - 1].start()
@@ -438,10 +445,10 @@
     c_s[1][3].wait_recv()
     prep(3, 1 - c, 1)
     multiply_in(3, 1)
+    far(1)
     c_s[1][1].wait_recv()
     prep(1, 1 - c, 1)
     multiply_in(1, 1)
-    far(1)
     sum_a[0].mid(3)
     sum_a[0].mid(1)
     ring_b[0][2].mid()
@@ -507,10 +514,10 @@
     for xx, cc in (
         (x, 1 - c),
         (x + 1 - 2 * lax.rem(x, 2), c),
-        (3 - x, c),
+        (x + 1 - 2 * lax.rem(x, 2), 1 - c),
         (wrap(x + 2), c),
         (wrap(x + 2), 1 - c),
-        (x + 1 - 2 * lax.rem(x, 2), 1 - c),
+        (3 - x, c),
         (3 - x, 1 - c),
     ):
         partners.append(xx * 2 + cc)
@@ -536,8 +543,7 @@
     contract = (((1,), (1,)), ((), ()))
     draft = lax.rem(lax.broadcasted_iota(jnp.int32, (128, 16), 0), 16)
     causal = lax.broadcasted_iota(jnp.int32, (128, 16), 1) <= draft
-    spot = pl.ds(pl.multiple_of(lax.rem(gy, 4) * 16, 16), 16)
-    home = g.at[lax.div(gy, 4), 0, 0, spot]
+    home = g.at[lax.div(gy, 4), lax.rem(x, 2), 0, 0, pl.ds(pl.multiple_of(c * 16, 16), 16)]
     k_in.wait()
     v_in.wait()
 
@@ -575,23 +581,66 @@
         result = (blend / total).astype(BF)
         return jnp.concatenate([result[h * 16 : (h + 1) * 16] for h in range(8)], axis=1)
 
-    home[...] = attend(gy)
     swap = []
-    for step, other in enumerate(partners):
+
+    def attend_step(step):
         pass_a[step].wait_recv()
         pass_b[step].wait_recv()
-        att[step] = attend(other)
-        swap.append(net.send(att.at[step], home, (me.gx, other)))
-
-    a1 = RingCast(net, [g.at[0, k, 0] for k in range(4)], zp, zm)
-    b1 = RingCast(net, [g.at[1, 0, k] for k in range(4)], yp, ym)
-    a2 = [RingCast(net, [g.at[0, j, k] for k in range(4)], yp, ym) for j in range(4)]
-    b2 = [RingCast(net, [g.at[1, k, j] for k in range(4)], zp, zm) for j in range(4)]
+        att[step] = attend(partners[step])
+        swap.append(net.send(att.at[step], home, (me.gx, partners[step])))
+
+    early = lax.div(x, 2)
+    half_of = (early, 1 - early)
+    rows_of_half = [pl.ds(pl.multiple_of(half * 64, 64), 64) for half in half_of]
+
+    class Gather:
+        def __init__(self, p):
+            buf = g.at[half_of[p]]
+            self.p = p
+            self.a1 = RingCast(net, [buf.at[0, k, 0] for k in range(4)], zp, zm)
+            self.b1 = RingCast(net, [buf.at[1, 0, k] for k in range(4)], yp, ym)
+            self.a2 = [RingCast(net, [buf.at[0, j, k] for k in range(4)], yp, ym) for j in range(4)]
+            self.b2 = [RingCast(net, [buf.at[1, k, j] for k in range(4)], zp, zm) for j in range(4)]
+
+        def begin(self, copies):
+            for copy in copies:
+                copy.wait_recv()
+            for ring in (self.a1, self.b1, self.a2[0], self.b2[0]):
+                ring.start()
+
+        def second(self):
+            self.a1.relay()
+            self.b1.relay()
+            for ring in (self.a2[1], self.b2[1], self.a2[3], self.b2[3]):
+                ring.start()
+
+        def third(self):
+            self.a2[0].relay()
+            self.b2[0].relay()
+            self.a1.far()
+            self.b1.far()
+            self.a2[2].start()
+            self.b2[2].start()
+
+        def fourth(self):
+            for ring in (self.a2[1], self.b2[1], self.a2[3], self.b2[3]):
+                ring.relay()
+
+        def last(self):
+            self.a2[2].relay()
+            self.b2[2].relay()
+
+        def complete(self, dy):
+            self.b2[dy].far()
+            if dy == 2:
+                for ring in self.a2:
+                    ring.far()
+
     mine = [lax.div(wrap(y + dy), 2) == c for dy in range(4)]
     pair = [
         [
             net.make(sib_send.at[dy, :, part], sib_recv.at[dy, :, part], me.sibling, False)
-            for part in span
+            for part in rows_of_half
         ]
         for dy in range(4)
     ]
@@ -601,7 +650,7 @@
                 net.make(out_x.at[dy, r - 1, part], in_x.at[dy, r - 1, part], me.at_x(r), False)
                 for r in (1, 2, 3)
             ]
-            for part in span
+            for part in rows_of_half
         ]
         for dy in range(4)
     ]
@@ -609,39 +658,47 @@
     def both_cores(dy, role, part):
         return sib_send[dy, role, part].astype(F32) + sib_recv[dy, role, part].astype(F32)
 
-    def multiply(half, dy):
+    def multiply(gather, dy):
+        p = gather.p
+        gather.complete(dy)
         rows = jnp.concatenate(
-            [g[half, wrap(x + role - z + 4), dy] for role in range(4)], axis=0
+            [
+                g[half_of[p], way, wrap(x + role - z + 4), dy]
+                for role in range(4)
+                for way in range(2)
+            ],
+            axis=0,
         )
         term = jnp.dot(rows, wo[...], preferred_element_type=F32).astype(BF)
         for role in range(4):
-            sib_send[dy, role, span[half], :] = term[role * 64 : (role + 1) * 64]
+            sib_send[dy, role, rows_of_half[p], :] = term[role * 64 : (role + 1) * 64]
 
         @pl.when(jnp.logical_not(mine[dy]))
         def _():
-            pair[dy][half].start()
-
-    def sum_start(half, dy):
+            pair[dy][p].start()
+
+    def sum_start(p, dy):
         @pl.when(mine[dy])
         def _():
-            pair[dy][half].wait_recv()
+            pair[dy][p].wait_recv()
             for r in (2, 1, 3):
-                out_x[dy, r - 1, span[half]] = both_cores(dy, r, span[half]).astype(BF)
-                sum_x[dy][half][r - 1].start()
+                out_x[dy, r - 1, rows_of_half[p]] = both_cores(dy, r, rows_of_half[p]).astype(BF)
+                sum_x[dy][p][r - 1].start()
 
     def sum_finish(dy):
         @pl.when(mine[dy])
         def _():
             base = lax.rem(wrap(y + dy), 2) * 128
-            for half in range(2):
-                for copy in sum_x[dy][half]:
-                    copy.wait_recv()
-                total = both_cores(dy, 0, span[half])
+            for copy in sum_x[dy][0] + sum_x[dy][1]:
+                copy.wait_recv()
+            for p in range(2):
+                part = rows_of_half[p]
+                total = both_cores(dy, 0, part)
                 for r in range(3):
-                    total = total + in_x[dy, r, span[half]].astype(F32)
-                rows = pl.ds(pl.multiple_of(base + half * 64, 64), 64)
+                    total = total + in_x[dy, r, part].astype(F32)
+                rows = pl.ds(pl.multiple_of(base + half_of[p] * 64, 64), 64)
                 out_ref[rows, :] = total.astype(BF)
-                for copy in sum_x[dy][half]:
+                for copy in sum_x[dy][p]:
                     copy.wait_send()
 
         @pl.when(jnp.logical_not(mine[dy]))
@@ -649,53 +706,42 @@
             for copy in pair[dy]:
                 copy.wait_send()
 
-    for copy in swap:
-        copy.wait_recv()
-    a1.start()
-    b1.start()
-    a2[0].start()
-    b2[0].start()
-    a1.relay()
-    b1.relay()
-    for ring in (a2[1], b2[1], a2[3], b2[3]):
-        ring.start()
-    a2[0].relay()
-    b2[0].relay()
-    a1.far()
-    b1.far()
-    a2[2].start()
-    b2[2].start()
+    ge, gl = Gather(0), Gather(1)
+    home[...] = attend(gy)
+    for step in range(4):
+        attend_step(step)
+    ge.begin(swap[:3])
+    attend_step(4)
+    ge.second()
+    attend_step(5)
+    ge.third()
+    attend_step(6)
+    ge.fourth()
+    gl.begin(swap[3:])
+    ge.last()
+    gl.second()
     wo_in.wait()
-    multiply(0, 0)
-    for ring in (a2[1], b2[1], a2[3], b2[3]):
-        ring.relay()
-    b2[0].far()
-    multiply(1, 0)
+    multiply(ge, 0)
+    gl.third()
     sum_start(0, 0)
-    a2[2].relay()
-    multiply(0, 1)
-    multiply(0, 3)
-    sum_start(1, 0)
-    b2[2].relay()
-    b2[1].far()
-    multiply(1, 1)
+    multiply(ge, 1)
+    multiply(ge, 3)
     sum_start(0, 1)
     sum_start(0, 3)
-    b2[3].far()
-    multiply(1, 3)
+    multiply(ge, 2)
+    gl.fourth()
+    sum_start(0, 2)
+    multiply(gl, 0)
+    gl.last()
+    sum_start(1, 0)
+    multiply(gl, 1)
     sum_start(1, 1)
-    for ring in a2:
-        ring.far()
-    multiply(0, 2)
+    multiply(gl, 3)
     sum_start(1, 3)
-    b2[2].far()
-    multiply(1, 2)
-    sum_start(0, 2)
+    multiply(gl, 2)
     sum_start(1, 2)
-    sum_finish(0)
-    sum_finish(1)
-    sum_finish(3)
-    sum_finish(2)
+    for dy in (0, 1, 3, 2):
+        sum_finish(dy)
     net.drain()
     assert net.count == COPIES, net.count
     assert len(local) == 8
@@ -727,7 +773,7 @@
             pltpu.VMEM((8, CTX), F32),
             pltpu.VMEM((128, CTX), F32),
             pltpu.VMEM((7, 16, 1024), BF),
-            pltpu.VMEM((2, 4, 4, 64, 1024), BF),
+            pltpu.VMEM((2, 2, 4, 4, 32, 1024), BF),
             pltpu.VMEM((1024, 512), BF),
             pltpu.VMEM((4, 4, 128, 512), BF),
             pltpu.VMEM((4, 4, 128, 512), BF),

time: 105 us -> 102 us (0.971)
  Pallas kernels: 102 us -> 98.4 us
    pallas_call x1, Pallas kernels: 102 us -> 98.4 us  [layer(): pl.pallas_call(layer_kernel, out_shape=jax.ShapeDtypeStruct((256, 512), B...]
where the time goes in v5:
time: 102 us; the launch traced here: 101 us
  Pallas kernels  98.4 us (96%)
  local copies, waits for them, and re-layouts  1.67 us (2%)
  between operations  1.31 us (1%)
    pallas_call x1, Pallas kernels, layer(): pl.pallas_call(layer_kernel, out_shape=jax.ShapeDtypeStruct((256, 512), B...  98.4 us

profile of v5, /device:TPU:1, one launch (start us, length us, event | category | flops | bytes accessed | tf_op | source)
XLA Modules:
  0.0 101.3 jit_solution(6875908641126984202)
XLA Ops:
  1.3 98.4 %layer.1 = bf16[256,512]{1,0:T(8,128)(2,1)} custom-call(bf16[2,128,512]{2,1,0:T(8,128)(2,1)} %bitcast.3, bf16[512]{0:T(512)(128)(2,1)} %gain_ref.1, bf16[512,1024]{1,0:T(8,128)(2,1)} %wq_h.1, bf16[512,128]{1,0:T(8,128)(2,1)} %wk_h.1, bf16[512,128]{1,0:T(8,128)(2,1)} %wv_h.1, bf16[1024,512]{1,0:T(8,128)(2,1)} %wo_h.1, f32[16,128]{1,0:T(8,128)} %constant.2.clone.freq_ref, ...), custom_call_target="tpu_custom_call" | custom-call | tf_op jit(solution)/shard_map/layer/pallas_call | solution.py:754
  99.7 1.7 %copy.15 = bf16[16,16,512]{2,1,0:T(8,128)(2,1)} copy(bf16[16,16,512]{2,1,0:T(8,128)(2,1)} %bitcast.2) | data formatting | bytes 524288

commit v6 on v5

--- a/solution.py
+++ b/solution.py
@@ -380,14 +380,14 @@
 
     def multiply_in(k, h):
         rows = scaled[k, h].reshape(256, 512)
+        term = jnp.dot(rows, w[:, :COLS], preferred_element_type=F32).astype(BF)
+        for j in range(4):
+            sum_a[h].out[k, wrap(j - y)] = term[j * 64 : (j + 1) * 64]
+        sum_a[h].block(k)
         term = jnp.dot(rows, w[:, COLS:], preferred_element_type=F32)
         for j in range(4):
             prod[h, k, j] = term[j * 64 : (j + 1) * 64]
         ring_b[h][k].start_far()
-        term = jnp.dot(rows, w[:, :COLS], preferred_element_type=F32).astype(BF)
-        for j in range(4):
-            sum_a[h].out[k, wrap(j - y)] = term[j * 64 : (j + 1) * 64]
-        sum_a[h].block(k)
         ring_b[h][k].start_near()
 
     def block_b(slot, h):

time: 102 us -> 101 us (level)
  no operation moved by 1% of the time
where the time goes in v6:
time: 101 us; the launch traced here: 100 us
  Pallas kernels  97.4 us (96%)
  local copies, waits for them, and re-layouts  1.67 us (2%)
  between operations  1.31 us (1%)
    pallas_call x1, Pallas kernels, layer(): pl.pallas_call(layer_kernel, out_shape=jax.ShapeDtypeStruct((256, 512), B...  97.4 us

profile of v6, /device:TPU:1, one launch (start us, length us, event | category | flops | bytes accessed | tf_op | source)
XLA Modules:
  0.0 100.4 jit_solution(8698230133671802151)
XLA Ops:
  1.3 97.4 %layer.1 = bf16[256,512]{1,0:T(8,128)(2,1)} custom-call(bf16[2,128,512]{2,1,0:T(8,128)(2,1)} %bitcast.3, bf16[512]{0:T(512)(128)(2,1)} %gain_ref.1, bf16[512,1024]{1,0:T(8,128)(2,1)} %wq_h.1, bf16[512,128]{1,0:T(8,128)(2,1)} %wk_h.1, bf16[512,128]{1,0:T(8,128)(2,1)} %wv_h.1, bf16[1024,512]{1,0:T(8,128)(2,1)} %wo_h.1, f32[16,128]{1,0:T(8,128)} %constant.2.clone.freq_ref, ...), custom_call_target="tpu_custom_call" | custom-call | tf_op jit(solution)/shard_map/layer/pallas_call | solution.py:754
  98.7 1.7 %copy.15 = bf16[16,16,512]{2,1,0:T(8,128)(2,1)} copy(bf16[16,16,512]{2,1,0:T(8,128)(2,1)} %bitcast.2) | data formatting | bytes 524288
